TPU v7x, 256 devices: a whole 4x4x8 slice. The times are simulated.
256 devices in a mesh: lat: 8 (over x, y_lo), lon: 32 (over z, y_hi, core).
Axes of the slice: x: 4, y: 4 (y_hi: 2, y_lo: 2; y = y_hi * 2 + y_lo), z: 8, core: 2. Of those that a mesh axis runs over, the one named last changes fastest.
Arguments:
- cells: bfloat16 [192, 768, 512], P('lat', 'lon'), may hold values from -6 to 6
- cotangent: bfloat16 [192, 768, 512], P('lat', 'lon'), may hold values from -3 to 3
- land: int32 [192, 768], P('lat', 'lon'), may hold values 0 or 1
- land_embed: float32 [512], replicated, may hold values from -3 to 3
- qkv_weight: bfloat16 [512, 1536], P('lon')
- proj_weight: bfloat16 [512, 512], P('lon'), may hold values from -0.25 to 0.25
- up_weight: bfloat16 [512, 2048], P('lon'), may hold values from -0.25 to 0.25
- down_weight: bfloat16 [2048, 512], P('lon'), may hold values from -0.125 to 0.125
- gain_one: bfloat16 [512], P('lon'), may hold values from 0.5 to 1.5
- gain_two: bfloat16 [512], P('lon'), may hold values from 0.5 to 1.5
Outputs:
- block_out: bfloat16 [192, 768, 512], P('lat', 'lon')
- grad_cells: bfloat16 [192, 768, 512], P('lat', 'lon')
- grad_qkv: float32 [512, 1536], P('lon')
- grad_proj: float32 [512, 512], P('lon')
- grad_up: float32 [512, 2048], P('lon')
- grad_down: float32 [2048, 512], P('lon')
- grad_gain_one: float32 [512], P('lon')
- grad_gain_two: float32 [512], P('lon')
All inputs are finite; a program needn't handle non-finite values. No bound on the sum of `land` on one device may be relied on, other than what follows from the above.
Results may differ from a plain program's by a relative error of at most 0.04.
The roundings to bfloat16 on the way count: a program that leaves them out, or rounds other values in their place, can miss the bound.
Values may be sent and summed in bfloat16 or wider, within the bound.
A program may use at most 128 MiB of HBM per device.

v0:
```python
import jax
import jax.numpy as jnp
from jax import lax
from jax.sharding import PartitionSpec as P

HEADS = 16
WIN = 12
SHIFT = 6


epsilon = 1e-05
negative = -1e30


def from_behind(array, axis, by):
    size = lax.axis_size(axis)
    return lax.ppermute(array, axis, [(i, (i + by) % size) for i in range(size)])


def float_einsum(form, left, right):
    return jnp.einsum(form, left, right, preferred_element_type=jnp.float32)


def left_product(left, right):
    return lax.dot_general(
        left, right, (((0,), (0,)), ((), ())), preferred_element_type=jnp.float32
    )


def right_product(left, right):
    return lax.dot_general(
        left, right, (((1,), (1,)), ((), ())), preferred_element_type=jnp.float32
    )


def layer_norm(values, gain):
    center = jnp.mean(values, axis=-1, keepdims=True)
    centred = values - center
    spread = jnp.mean(centred * centred, axis=-1, keepdims=True)
    inverse = lax.rsqrt(spread + epsilon)
    normed = centred * inverse
    return (normed, inverse, (normed * gain).astype(jnp.bfloat16))


def norm_back(upstream, normed, inverse, gain):
    scaled = upstream * gain
    inner = (
        scaled
        - jnp.mean(scaled, axis=-1, keepdims=True)
        - normed * jnp.mean(scaled * normed, axis=-1, keepdims=True)
    )
    return (inner * inverse, jnp.sum(upstream * normed, axis=0))


def windowed(field):
    height, breadth, depth = field.shape
    shaped = field.reshape(height // WIN, WIN, breadth // WIN, WIN, depth)
    return shaped.transpose(0, 2, 1, 3, 4).reshape(height * breadth, depth)


def unwindow(tokens, height, breadth):
    depth = tokens.shape[1]
    shaped = tokens.reshape(height // WIN, breadth // WIN, WIN, WIN, depth)
    return shaped.transpose(0, 2, 1, 3, 4).reshape(height, breadth, depth)


def gelu_slope(values):
    return (
        0.5 * (1.0 + lax.erf(values * 0.7071067811865476))
        + values * jnp.exp(-0.5 * values * values) * 0.3989422804014327
    )


def block_pass(field, upstream, rows_global, limit, weights, settle, refetch):
    height, breadth, width = field.shape
    head_size = width // HEADS
    scale = head_size ** (-0.5)
    tokens = windowed(field)
    count_tokens = tokens.shape[0]
    groups = count_tokens // (WIN * WIN)
    flags = jnp.broadcast_to(
        (rows_global >= limit).astype(jnp.int32)[:, None, None], (height, breadth, 1)
    )
    region = windowed(flags).reshape(groups, WIN * WIN)
    qkv_weight, proj_weight, up_weight, down_weight, gain_one, gain_two = weights
    inputs = tokens.astype(jnp.float32)
    normed_one, inverse_one, hidden_one = layer_norm(inputs, gain_one.astype(jnp.float32))
    packed = jnp.dot(hidden_one, qkv_weight, preferred_element_type=jnp.float32).astype(
        jnp.bfloat16
    )
    split = packed.reshape(groups, WIN * WIN, 3, HEADS, head_size)
    query = split[:, :, 0]
    keyed = split[:, :, 1]
    valued = split[:, :, 2]
    scores = float_einsum("wqhd,wkhd->whqk", query, keyed) * scale
    allowed = region[:, None, :, None] == region[:, None, None, :]
    scores = jnp.where(allowed, scores, negative)
    highest = jnp.max(scores, axis=-1, keepdims=True)
    raised = jnp.exp(scores - highest)
    probs = raised / jnp.sum(raised, axis=-1, keepdims=True)
    probs_low = probs.astype(jnp.bfloat16)
    attended = (
        float_einsum("whqk,wkhd->wqhd", probs_low, valued)
        .astype(jnp.bfloat16)
        .reshape(count_tokens, width)
    )
    middle = inputs + jnp.dot(attended, proj_weight, preferred_element_type=jnp.float32)
    normed_two, inverse_two, hidden_two = layer_norm(middle, gain_two.astype(jnp.float32))
    raised_up = jnp.dot(hidden_two, up_weight, preferred_element_type=jnp.float32)
    active = jax.nn.gelu(raised_up, approximate=False).astype(jnp.bfloat16)
    output = (middle + jnp.dot(active, down_weight, preferred_element_type=jnp.float32)).astype(
        jnp.bfloat16
    )
    qkv_back, proj_back, up_back, down_back, gain_one_back, gain_two_back = refetch(weights)
    incoming = windowed(upstream)
    grad_down = settle(lambda start, count: left_product(active, incoming), active.shape[1])
    grad_active = right_product(incoming, down_back)
    grad_raised = (grad_active * gelu_slope(raised_up)).astype(jnp.bfloat16)
    grad_up = settle(lambda start, count: left_product(hidden_two, grad_raised), width)
    grad_hidden_two = right_product(grad_raised, up_back)
    grad_middle_norm, gain_two_sum = norm_back(
        grad_hidden_two, normed_two, inverse_two, gain_two_back.astype(jnp.float32)
    )
    grad_gain_two = settle(lambda start, count: gain_two_sum, width)
    grad_middle = incoming.astype(jnp.float32) + grad_middle_norm
    grad_middle_low = grad_middle.astype(jnp.bfloat16)
    grad_proj = settle(lambda start, count: left_product(attended, grad_middle_low), width)
    grad_attended = (
        right_product(grad_middle_low, proj_back)
        .astype(jnp.bfloat16)
        .reshape(groups, WIN * WIN, HEADS, head_size)
    )
    grad_probs = float_einsum("wqhd,wkhd->whqk", grad_attended, valued)
    grad_valued = float_einsum("whqk,wqhd->wkhd", probs_low, grad_attended)
    grad_scores = probs * (grad_probs - jnp.sum(grad_probs * probs, axis=-1, keepdims=True)) * scale
    grad_scores_low = grad_scores.astype(jnp.bfloat16)
    grad_query = float_einsum("whqk,wkhd->wqhd", grad_scores_low, keyed)
    grad_keyed = float_einsum("whqk,wqhd->wkhd", grad_scores_low, query)
    grad_packed = (
        jnp.stack([grad_query, grad_keyed, grad_valued], axis=2)
        .reshape(count_tokens, 3 * width)
        .astype(jnp.bfloat16)
    )
    grad_qkv = settle(lambda start, count: left_product(hidden_one, grad_packed), width)
    grad_hidden_one = right_product(grad_packed, qkv_back)
    grad_inputs_norm, gain_one_sum = norm_back(
        grad_hidden_one, normed_one, inverse_one, gain_one_back.astype(jnp.float32)
    )
    grad_gain_one = settle(lambda start, count: gain_one_sum, width)
    grad_inputs = (grad_middle + grad_inputs_norm).astype(jnp.bfloat16)
    grads = (grad_qkv, grad_proj, grad_up, grad_down, grad_gain_one, grad_gain_two)
    return (unwindow(output, height, breadth), unwindow(grad_inputs, height, breadth), grads)


def to_shifted(stacked):
    lower = from_behind(stacked[:, :SHIFT], "lat", -1)
    rows_done = jnp.concatenate([stacked[:, SHIFT:], lower], axis=1)
    right = from_behind(rows_done[:, :, :SHIFT], "lon", -1)
    return jnp.concatenate([rows_done[:, :, SHIFT:], right], axis=2)


def from_shifted(stacked):
    left = from_behind(stacked[:, :, -SHIFT:], "lon", 1)
    cols_done = jnp.concatenate([left, stacked[:, :, :-SHIFT]], axis=2)
    upper = from_behind(cols_done[:, -SHIFT:], "lat", 1)
    return jnp.concatenate([upper, cols_done[:, :-SHIFT]], axis=1)


def body(
    cells,
    cotangent,
    land,
    land_embed,
    qkv_weight,
    proj_weight,
    up_weight,
    down_weight,
    gain_one,
    gain_two,
):
    height = cells.shape[0]
    start = (
        cells.astype(jnp.float32) + land[:, :, None].astype(jnp.float32) * land_embed[None, None, :]
    ).astype(jnp.bfloat16)
    rows_global = lax.axis_index("lat") * height + jnp.arange(height, dtype=jnp.int32)
    limit = height * lax.axis_size("lat") - SHIFT
    weights = (
        lax.all_gather(qkv_weight, "lon", axis=0, tiled=True),
        lax.all_gather(proj_weight, "lon", axis=0, tiled=True),
        lax.all_gather(up_weight, "lon", axis=0, tiled=True),
        lax.all_gather(down_weight, "lon", axis=0, tiled=True),
        lax.all_gather(gain_one, "lon", axis=0, tiled=True),
        lax.all_gather(gain_two, "lon", axis=0, tiled=True),
    )

    def refetch(unused):
        return unused

    def settle(function, total):
        return function(0, total)

    moved_field = to_shifted(start[None])[0]
    moved_cot = to_shifted(cotangent[None])[0]
    output, grad_inputs, grads = block_pass(
        moved_field, moved_cot, rows_global, limit, weights, settle, refetch
    )
    block_out = from_shifted(output[None])[0]
    grad_cells = from_shifted(grad_inputs[None])[0]
    shares = (
        lax.psum_scatter(grads[0], "lon", scatter_dimension=0, tiled=True),
        lax.psum_scatter(grads[1], "lon", scatter_dimension=0, tiled=True),
        lax.psum_scatter(grads[2], "lon", scatter_dimension=0, tiled=True),
        lax.psum_scatter(grads[3], "lon", scatter_dimension=0, tiled=True),
        lax.psum_scatter(grads[4], "lon", scatter_dimension=0, tiled=True),
        lax.psum_scatter(grads[5], "lon", scatter_dimension=0, tiled=True),
    )
    totals = lax.psum((shares[0], shares[1], shares[2], shares[3], shares[4], shares[5]), "lat")
    return (block_out, grad_cells, totals[0], totals[1], totals[2], totals[3], totals[4], totals[5])


def solution(mesh):
    placed = (
        P("lat", "lon", None),
        P("lat", "lon", None),
        P("lat", "lon"),
        P(),
        P("lon", None),
        P("lon", None),
        P("lon", None),
        P("lon", None),
        P("lon"),
        P("lon"),
    )
    return jax.shard_map(
        body,
        mesh=mesh,
        in_specs=placed,
        out_specs=(
            P("lat", "lon", None),
            P("lat", "lon", None),
            P("lon", None),
            P("lon", None),
            P("lon", None),
            P("lon", None),
            P("lon"),
            P("lon"),
        ),
        check_vma=False,
    )
```

profile of v0, /device:TPU:32, one launch (start us, length us, event | category | flops | bytes accessed | tf_op | source)
XLA Modules:
  0.0 919.2 jit_solution(12342291435219428847)
XLA Ops:
  7.2 0.7 all-gather.4.cloned.1.call-update
  8.0 0.7 all-gather.6.cloned.1.call-update
  8.7 0.9 slice.86
  9.7 3.8 collective-permute-start.4
  13.5 0.7 convert_element_type.105
  14.2 1.3 fusion.57
  16.3 46.7 %all_gather.20 = bf16[512,512]{1,0:T(8,128)(2,1)} all-gather(bf16[16,512]{1,0:T(8,128)(2,1)} %param.15), channel_id=1, replica_groups=mesh['lat'=8,'lon'=32] {'lon'}, dimensions={0}, use_global_device_ids=true | all-gather | bytes 540672 | tf_op jit(solution)/shard_map/all_gather | solution.py:189
  63.2 1.0 slice.85
  66.0 59.3 %all-reduce.7 = (bf16[512]{0:T(512)(128)(2,1)S(1)}, bf16[512]{0:T(512)(128)(2,1)S(1)}) all-reduce(bf16[512]{0:T(512)(128)(2,1)S(1)} %dynamic-update-slice, bf16[512]{0:T(512)(128)(2,1)S(1)} %dynamic-update-slice.1), channel_id=1, replica_groups=mesh['lat'=8,'lon'=32] {'lon'}, use_global_device_ids=true, to_apply=%add | all-reduce | flops 1024 | bytes 4096
  125.9 0.7 pad_maximum_fusion.3
  126.6 5.1 collective-permute-start.5
  131.7 1.0 collective-permute-start.1
  133.0 4.1 collective-permute-done.1
  137.8 1.0 multiply_reduce_fusion.1
  138.7 1.8 pad_maximum_fusion.2
  140.6 1.4 reshape_squeeze.4
  142.0 0.9 reshape.156
  143.6 1.0 convert_element_type.132
  144.9 2.9 convolution_convert_fusion
  147.9 2.3 copy.54
  150.2 6.5 reshape.153
  156.7 2.6 fusion.76
  159.3 8.9 fusion.78
  168.8 4.5 fusion.49
  173.4 0.9 copy.59
  174.3 0.7 reshape.154
  176.0 14.6 %fusion.8 = (bf16[576,2048]{1,0:T(8,128)(2,1)}, f32[576,2048]{1,0:T(8,128)}) fusion(bf16[512,2048]{1,0:T(8,128)(2,1)} %all-gather.6.cloned.1.call-done, f32[576,512]{1,0:T(8,128)S(1)} %get-tuple-element.32, f32[512]{0:T(512)} %convert_element_type.119, f32[576]{0:T(1024)S(1)} %add_rsqrt_fusion.1, f32[576]{0:T(1024)S(1)} %broadcast_multiply_fusion.5), kind=kOutput, calls=%fused_computation.13 | convolution fusion | flops 1285816320 | bytes 10361344 | tf_op jit(solution)/shard_map/dot_general | solution.py:109
  190.5 59.5 %all-gather.8.cloned.1.call-done = bf16[2048,512]{1,0:T(8,128)(2,1)} async-done(((bf16[64,512]{1,0:T(8,128)(2,1)}), bf16[2048,512]{1,0:T(8,128)(2,1)}) %all-gather.8.cloned.1.call-update) | async-done | bytes 2097168 | tf_op jit(solution)/shard_map/all_gather | solution.py:191
  250.0 4.8 fusion.14
  254.9 2.2 multiply_reduce_fusion.2
  258.2 1.4 convolution_convert_fusion.1
  259.5 2.2 copy.62
  261.7 4.0 reshape.157
  265.7 6.7 fusion.37
  272.4 5.1 fusion.53
  277.5 16.2 %fusion.40 = bf16[4,144,1,16,32]{1,4,3,0,2:T(8,128)(2,1)} fusion(f32[4,16,144,144]{2,3,1,0:T(8,128)} %fusion.53, bf16[4,144,1,16,32]{1,0,4,3,2:T(4,128)(2,1)} %get-tuple-element.24, f32[4,16,144,144]{2,3,1,0:T(8,128)} %get-tuple-element.30, f32[4,16,144]{2,1,0:T(8,128)} %copy-done.20), kind=kOutput, calls=%fused_computation.48 | convolution fusion | flops 94233744 | bytes 11833344 | tf_op jit(solution)/shard_map/whqk,wkhd->wqhd/dot_general | solution.py:21
  293.7 16.0 %fusion.43 = bf16[4,144,1,16,32]{1,4,3,0,2:T(8,128)(2,1)} fusion(f32[4,16,144,144]{2,3,1,0:T(8,128)} %fusion.53, bf16[4,144,1,16,32]{1,0,4,3,2:T(4,128)(2,1)} %get-tuple-element.25, f32[4,16,144,144]{2,3,1,0:T(8,128)} %get-tuple-element.30, f32[4,16,144]{2,1,0:T(8,128)} %copy-done.20), kind=kOutput, calls=%fused_computation.49 | convolution fusion | flops 94233744 | bytes 11833344 | tf_op jit(solution)/shard_map/whqk,wqhd->wkhd/dot_general | solution.py:21
  309.7 2.6 maximum_convert_fusion
  312.2 4.9 copy.68
  317.1 6.4 convert_element_type.129
  323.5 5.0 fusion.80
  328.5 5.6 fusion.74
  334.2 5.6 fusion.81
  339.8 2.7 fusion.65
  342.6 4.6 fusion.52
  347.2 1.2 reshape.155
  348.4 1.0 copy.60
  349.4 1.3 broadcast_in_dim_reshape.6
  350.7 0.7 slice.83
  351.7 4.3 multiply_reduce_fusion.3
  357.2 2.0 collective-permute-done.2
  359.2 0.8 pad_maximum_fusion.6
  360.7 87.7 %reduce-scatter.5.cloned.1.call-done = f32[16,1536]{1,0:T(8,128)} async-done(((f32[512,1536]{1,0:T(8,128)}), f32[16,1536]{1,0:T(8,128)}) %reduce-scatter.5.cloned.1.call-update) | async-done | bytes 98320 | tf_op jit(solution)/shard_map/reduce_scatter | solution.py:210
  448.4 130.4 %reduce-scatter.9.cloned.1.call-done = f32[16,2048]{1,0:T(8,128)} async-done(((f32[512,2048]{1,0:T(8,128)}), f32[16,2048]{1,0:T(8,128)}) %reduce-scatter.9.cloned.1.call-update) | async-done | bytes 131088 | tf_op jit(solution)/shard_map/reduce_scatter | solution.py:212
  578.8 129.7 %reduce-scatter.11.cloned.1.call-done = f32[64,512]{1,0:T(8,128)} async-done(((f32[2048,512]{1,0:T(8,128)}), f32[64,512]{1,0:T(8,128)}) %reduce-scatter.11.cloned.1.call-update) | async-done | bytes 131088 | tf_op jit(solution)/shard_map/reduce_scatter | solution.py:213
  709.9 57.8 %all-reduce.4 = (f32[512]{0:T(512)S(1)}, f32[512]{0:T(512)S(1)}) all-reduce(f32[512]{0:T(512)S(1)} %copy-done.14, f32[512]{0:T(512)S(1)} %copy-done.13), channel_id=6, replica_groups=mesh['lat'=8,'lon'=32] {'lon'}, use_global_device_ids=true, to_apply=%region_20.21.clone | all-reduce | flops 1024 | bytes 8192
  767.8 1.9 fusion.61
  769.7 1.0 fusion.59
  770.7 55.6 %reduce-scatter.7.cloned.1.call-done = f32[16,512]{1,0:T(8,128)} async-done(((f32[512,512]{1,0:T(8,128)}), f32[16,512]{1,0:T(8,128)}) %reduce-scatter.7.cloned.1.call-update) | async-done | bytes 32784 | tf_op jit(solution)/shard_map/reduce_scatter | solution.py:211
  826.2 34.2 %all-reduce.5 = (f32[16,512]{1,0:T(8,128)}, f32[16]{0:T(128)}, f32[16]{0:T(128)}) all-reduce(f32[16,512]{1,0:T(8,128)} %reduce-scatter.7.cloned.1.call-done, f32[16]{0:T(128)S(1)} %dynamic-slice.3, f32[16]{0:T(128)S(1)} %dynamic-slice.5), channel_id=1, replica_groups=mesh['lat'=8,'lon'=32] {'lat'}, use_global_device_ids=true, to_apply=%region_14.15 | all-reduce | flops 8224 | bytes 65792 | tf_op jit(solution)/shard_map/psum | solution.py:217
  860.4 47.2 %all-reduce.10.cloned.1.call-done = (f32[16,1536]{1,0:T(8,128)}, f32[16,2048]{1,0:T(8,128)}, f32[64,512]{1,0:T(8,128)}) async-done(((f32[16,1536]{1,0:T(8,128)}, f32[16,2048]{1,0:T(8,128)}, f32[64,512]{1,0:T(8,128)}), (f32[16,1536]{1,0:T(8,128)}, f32[16,2048]{1,0:T(8,128)}, f32[64,512]{1,0:T(8,128)})) %all-reduce.10.cloned.1.call-update) | async-done | bytes 360464 | tf_op jit(solution)/shard_map/psum | solution.py:217
  907.5 1.5 copy.112
  909.1 1.6 copy.113
  910.6 1.6 copy.114
  (115 shorter events, 10.5 us)
Async XLA Ops:
  7.2 57.1 %copy-start.15 = (u32[256]{0:T(256)S(1)}, u32[256]{0:T(256)}, u32[]{:S(2)}) copy-start(u32[256]{0:T(256)} %constant.105) | copy-start | bytes 3076
  7.2 58.3 %copy-start.17 = (bf16[16]{0:T(256)(128)(2,1)S(1)}, bf16[16]{0:T(256)(128)(2,1)}, u32[]{:S(2)}) copy-start(bf16[16]{0:T(256)(128)(2,1)} %param.18) | copy-start | bytes 100
  7.2 58.6 %copy-start.18 = (bf16[16]{0:T(256)(128)(2,1)S(1)}, bf16[16]{0:T(256)(128)(2,1)}, u32[]{:S(2)}) copy-start(bf16[16]{0:T(256)(128)(2,1)} %param.19) | copy-start | bytes 100
  7.2 137.7 %all-gather.4.cloned.1.call-start = ((), (), s32[]{:S(2)}) async-start(), calls=%async_computation.4 | async-start | bytes 1622016 | tf_op jit(solution)/shard_map/all_gather | solution.py:188
  7.9 168.0 %all-gather.6.cloned.1.call-start = ((), (), s32[]{:S(2)}) async-start(), calls=%async_computation.5 | async-start | bytes 2162688 | tf_op jit(solution)/shard_map/all_gather | solution.py:190
  8.7 241.3 %all-gather.8.cloned.1.call-start = ((), (), s32[]{:S(2)}) async-start(), calls=%async_computation.6 | async-start | bytes 2162688 | tf_op jit(solution)/shard_map/all_gather | solution.py:191
  9.7 116.3 %collective-permute-start.4 = (bf16[1,6,24,512]{3,2,1,0:T(8,128)(2,1)S(1)}, bf16[1,6,24,512]{3,2,1,0:T(8,128)(2,1)S(1)}, u32[]{:S(2)}, u32[]{:S(2)}) collective-permute-start(bf16[1,6,24,512]{3,2,1,0:T(8,128)(2,1)S(1)} %slice.86), channel_id=1, source_target_pairs={{0,224},{32,0},{64,32},{96,64},{128,96},{160,128},{192,160},{224,1... | collective-permute-start | bytes 442376 | tf_op jit(solution)/shard_map/ppermute | solution.py:17
  15.5 116.2 %collective-permute-start = (bf16[1,6,24,512]{3,2,1,0:T(8,128)(2,1)S(1)}, bf16[1,6,24,512]{3,2,1,0:T(8,128)(2,1)S(1)}, u32[]{:S(2)}, u32[]{:S(2)}) collective-permute-start(bf16[1,6,24,512]{3,2,1,0:T(8,128)(2,1)S(1)} %slice.77), channel_id=1, source_target_pairs={{0,224},{32,0},{64,32},{96,64},{128,96},{160,128},{192,160},{224,1... | collective-permute-start | bytes 442376 | tf_op jit(solution)/shard_map/ppermute | solution.py:17
  16.1 432.4 %reduce-scatter.5.cloned.1.call-start = ((), (), s32[]{:S(2)}) async-start(), calls=%async_computation.7 | async-start | bytes 3244032 | tf_op jit(solution)/shard_map/reduce_scatter | solution.py:210
  126.6 12.1 %collective-permute-start.5 = (bf16[1,24,6,512]{3,2,1,0:T(8,128)(2,1)}, bf16[1,24,6,512]{3,2,1,0:T(8,128)(2,1)}, u32[]{:S(2)}, u32[]{:S(2)}) collective-permute-start(bf16[1,24,6,512]{3,2,1,0:T(8,128)(2,1)} %pad_maximum_fusion.3), channel_id=1, source_target_pairs={{0,31},{1,0},{2,1},{3,2},{4,3},{5,4},{6,5},{7,6},{8,7},{9,8},{10,9... | collective-permute-start | bytes 442376 | tf_op jit(solution)/shard_map/ppermute | solution.py:17
  131.7 5.5 collective-permute-start.1
  140.6 2.4 copy-start.9
  143.2 1.7 copy-start.10
  144.9 3.0 copy-start
  159.3 9.6 %copy-start.2 = (bf16[4,144,1,16,32]{1,0,4,3,2:T(4,128)(2,1)S(1)}, bf16[4,144,1,16,32]{1,0,4,3,2:T(4,128)(2,1)}, u32[]{:S(2)}) copy-start(bf16[4,144,1,16,32]{1,0,4,3,2:T(4,128)(2,1)} %get-tuple-element.26) | copy-start | bytes 1769476
  168.2 0.6 copy-start.20
  173.4 1.6 copy-start.1
  173.4 1.6 copy-start.6
  175.0 15.5 %copy-start.5 = (bf16[576,512]{0,1:T(8,128)(2,1)}, bf16[576,512]{0,1:T(8,128)(2,1)S(1)}, u32[]{:S(2)}) copy-start(bf16[576,512]{0,1:T(8,128)(2,1)S(1)} %reshape.154) | copy-start | bytes 1769476
  250.0 4.9 copy-start.12
  250.0 4.9 copy-start.16
  254.9 2.2 copy-start.19
  254.9 2.2 copy-start.8
  257.1 1.0 copy-start.7
  265.7 6.7 copy-start.3
  265.7 6.7 copy-start.4
  328.5 250.3 %reduce-scatter.9.cloned.1.call-start = ((), (), s32[]{:S(2)}) async-start(), calls=%async_computation.9 | async-start | bytes 4325376 | tf_op jit(solution)/shard_map/reduce_scatter | solution.py:212
  334.1 374.4 %reduce-scatter.11.cloned.1.call-start = ((), (), s32[]{:S(2)}) async-start(), calls=%async_computation.10 | async-start | bytes 4325376 | tf_op jit(solution)/shard_map/reduce_scatter | solution.py:213
  339.8 486.5 %reduce-scatter.7.cloned.1.call-start = ((), (), s32[]{:S(2)}) async-start(), calls=%async_computation.8 | async-start | bytes 1081344 | tf_op jit(solution)/shard_map/reduce_scatter | solution.py:211
  342.5 565.0 %all-reduce.10.cloned.1.call-start = ((), (), s32[]{:S(2)}) async-start(), calls=%async_computation.11 | async-start | bytes 720896 | tf_op jit(solution)/shard_map/psum | solution.py:217
  347.2 4.5 copy-start.11
  351.4 7.8 collective-permute-start.2
  356.4 353.5 %copy-start.13 = (f32[512]{0:T(512)S(1)}, f32[512]{0:T(512)}, u32[]{:S(2)}) copy-start(f32[512]{0:T(512)} %get-tuple-element.8) | copy-start | bytes 6148
  356.4 353.5 %copy-start.14 = (f32[512]{0:T(512)S(1)}, f32[512]{0:T(512)}, u32[]{:S(2)}) copy-start(f32[512]{0:T(512)} %get-tuple-element.10) | copy-start | bytes 6148
  356.8 351.7 %collective-permute-start.6 = (bf16[1,24,6,512]{3,2,1,0:T(8,128)(2,1)S(1)}, bf16[1,24,6,512]{3,2,1,0:T(8,128)(2,1)S(1)}, u32[]{:S(2)}, u32[]{:S(2)}) collective-permute-start(bf16[1,24,6,512]{3,2,1,0:T(8,128)(2,1)S(1)} %slice.89), channel_id=1, source_target_pairs={{0,1},{1,2},{2,3},{3,4},{4,5},{5,6},{6,7},{7,8},{8,9},{9,10},{10,1... | collective-permute-start | bytes 442376 | tf_op jit(solution)/shard_map/ppermute | solution.py:17
  360.1 407.8 %collective-permute-start.3 = (bf16[1,6,24,512]{3,2,1,0:T(8,128)(2,1)S(1)}, bf16[1,6,24,512]{3,2,1,0:T(8,128)(2,1)S(1)}, u32[]{:S(2)}, u32[]{:S(2)}) collective-permute-start(bf16[1,6,24,512]{3,2,1,0:T(8,128)(2,1)S(1)} %pad_maximum_fusion.6), channel_id=1, source_target_pairs={{0,32},{32,64},{64,96},{96,128},{128,160},{160,192},{192,224},{224... | collective-permute-start | bytes 442376 | tf_op jit(solution)/shard_map/ppermute | solution.py:17
  708.6 61.1 %collective-permute-start.7 = (bf16[1,6,24,512]{3,2,1,0:T(8,128)(2,1)S(1)}, bf16[1,6,24,512]{3,2,1,0:T(8,128)(2,1)S(1)}, u32[]{:S(2)}, u32[]{:S(2)}) collective-permute-start(bf16[1,6,24,512]{3,2,1,0:T(8,128)(2,1)S(1)} %pad_maximum_fusion.5), channel_id=1, source_target_pairs={{0,32},{32,64},{64,96},{96,128},{128,160},{160,192},{192,224},{224... | collective-permute-start | bytes 442376 | tf_op jit(solution)/shard_map/ppermute | solution.py:17
Sparse Core Ops, SparseCore 0:
  10.8 80.4 all-gather.3
  94.1 76.4 all-gather.5
  173.5 76.5 all-gather.7
  328.6 119.7 reduce-scatter.4
  453.1 125.6 reduce-scatter.8
  582.9 125.5 reduce-scatter.10
  713.1 113.0 reduce-scatter.6
  829.1 78.4 all-reduce.9
where the time goes:
time: 925 us; the launch traced here: 919 us
  waiting for transfers between devices  518 us (56%)
  blocking collectives  198 us (21%)
  matrix products  112 us (12%)
  local copies, waits for them, and re-layouts  48.3 us (5%)
  between operations  16.2 us (2%)
  other arithmetic  14.7 us (2%)
  starting transfers between devices  12.8 us (1%)
    reduce_scatter x1, waiting for transfers between devices, body(): lax.psum_scatter(grads[2], 'lon', scatter_dimension=0, tiled=True)  130 us
    reduce_scatter x1, waiting for transfers between devices, body(): lax.psum_scatter(grads[3], 'lon', scatter_dimension=0, tiled=True)  130 us
    unnamed x2, blocking collectives  117 us
    reduce_scatter x1, waiting for transfers between devices, body(): lax.psum_scatter(grads[0], 'lon', scatter_dimension=0, tiled=True)  87.7 us
    all_gather x1, waiting for transfers between devices, body(): lax.all_gather(down_weight, 'lon', axis=0, tiled=True)  59.5 us
    reduce_scatter x1, waiting for transfers between devices, body(): lax.psum_scatter(grads[1], 'lon', scatter_dimension=0, tiled=True)  55.6 us
    dot_general x5, matrix products, float_einsum(): return jnp.einsum(form, left, right, preferred_element_type=jnp.float32)  48.5 us
    psum x1, waiting for transfers between devices, body(): lax.psum((shares[0], shares[1], shares[2], shares[3], shares[4], shares[5...  47.2 us
  transfers between devices with their start and end apart: 16, of which 8 were waited for; matrix products, arithmetic and copies ran while one was open for 10% of the time, Pallas kernels for 0%

commit v1 on v0

v1 whole, which is shorter than its diff:
```python
import functools

import jax
import jax.numpy as jnp
from jax import lax
from jax.experimental import pallas as pl
from jax.experimental.pallas import tpu as pltpu
from jax.sharding import PartitionSpec as P

HEADS = 16
WIN = 12
SHIFT = 6
EPS = 1e-5
NEG = -1e30
TOK = WIN * WIN
QUAD = SHIFT * SHIFT
PADQ = 48
GROUP = 256
F32 = jnp.float32
BF16 = jnp.bfloat16
MESH = pl.DeviceIdType.MESH


def nn(a, b):
    return lax.dot_general(a, b, (((1,), (0,)), ((), ())), preferred_element_type=F32)


def nt(a, b):
    return lax.dot_general(a, b, (((1,), (1,)), ((), ())), preferred_element_type=F32)


def tn(a, b):
    return lax.dot_general(a, b, (((0,), (0,)), ((), ())), preferred_element_type=F32)


def layer_norm(x):
    centred = x - jnp.mean(x, axis=-1, keepdims=True)
    spread = jnp.mean(centred * centred, axis=-1, keepdims=True)
    inverse = lax.rsqrt(spread + EPS)
    return centred * inverse, inverse


def norm_back(upstream, normed, inverse, gain):
    scaled = upstream * gain
    inner = (
        scaled
        - jnp.mean(scaled, axis=-1, keepdims=True)
        - normed * jnp.mean(scaled * normed, axis=-1, keepdims=True)
    )
    return inner * inverse, jnp.sum(upstream * normed, axis=0, keepdims=True)


class Place:
    def __init__(self, lats, lons):
        self.lats, self.lons, self.rings = lats, lons, lons // 4
        self.lat = lax.axis_index("lat")
        self.lon = lax.axis_index("lon")
        self.z = self.lon // 4
        self.yh = (self.lon // 2) % 2
        self.core = self.lon % 2
        self.sibling = (self.lat, self.lon + 1 - 2 * self.core)
        near = self.lat + 1 - 2 * (self.lat % 2)
        self.partner = (near, self.z * 4 + (1 - self.yh) * 2 + self.core)

    def along_z(self, by):
        z = (self.z + by + self.rings) % self.rings
        return (self.lat, z * 4 + self.yh * 2 + self.core)

    def moved(self, by_lat, by_lon):
        lat = (self.lat + by_lat + self.lats) % self.lats
        lon = (self.lon + by_lon + self.lons) % self.lons
        return (lat, lon)

    def in_plane(self, by):
        index = (self.yh * self.lats + self.lat + by) % (2 * self.lats)
        return index // self.lats, index % self.lats

    def plane_device(self, by):
        yh, lat = self.in_plane(by)
        return (lat, self.z * 4 + yh * 2 + self.core)


class Wires:
    def __init__(self, send, recv):
        self.send, self.recv, self.used, self.sent = send, recv, 0, []

    def take(self, count):
        first = self.used
        self.used += count
        return first

    def copy(self, src, dst, index, device):
        return pltpu.make_async_remote_copy(
            src_ref=src,
            dst_ref=dst,
            send_sem=self.send.at[index],
            recv_sem=self.recv.at[index],
            device_id=device,
            device_id_type=MESH,
        )

    def start(self, src, dst, index, device, until=None):
        self.copy(src, dst, index, device).start()
        if until is not None:
            self.sent.append((until, index))

    def landed(self, ref, index, device):
        self.copy(ref, ref, index, device).wait_recv()

    def finish(self, device):
        for view, index in self.sent:
            ref = view()
            self.copy(ref, ref, index, device).wait_send()


class Gather:
    def __init__(self, place, wires, shard, whole):
        self.p, self.w, self.shard, self.whole = place, wires, shard, whole
        self.right, self.left = place.rings // 2, place.rings // 2 - 1
        self.base = wires.take(1 + self.right + self.left + place.rings)

    def slot(self, rel, core):
        p = self.p
        return self.whole.at[(p.z - rel + p.rings) % p.rings, :, core]

    def begin(self):
        p = self.p
        here = self.whole.at[p.z, p.yh, p.core]
        here[...] = self.shard[...]
        self.w.start(self.shard, here, self.base, p.partner, lambda: self.shard)

    def share(self, rel):
        p = self.p
        index = self.base + 1 + self.right + self.left + rel
        block = self.slot(rel, p.core)
        self.w.start(block, block, index, p.sibling, lambda: self.whole.at[0, :, 0])

    def tick(self, step):
        p = self.p
        if step == 0:
            self.w.landed(self.whole.at[p.z, 1 - p.yh, p.core], self.base, p.partner)
            arrived = (0,)
        else:
            arrived = []
            self.w.landed(self.slot(step, p.core), self.base + step, p.along_z(-1))
            arrived.append(step)
            if step <= self.left:
                index = self.base + self.right + step
                self.w.landed(self.slot(p.rings - step, p.core), index, p.along_z(1))
                arrived.append(p.rings - step)
        if step < self.right:
            block = self.slot(step, p.core)
            index = self.base + 1 + step
            self.w.start(block, block, index, p.along_z(1), lambda: self.whole.at[0, :, 0])
        if step < self.left:
            block = self.slot((p.rings - step) % p.rings, p.core)
            index = self.base + 1 + self.right + step
            self.w.start(block, block, index, p.along_z(-1), lambda: self.whole.at[0, :, 0])
        for rel in arrived:
            self.share(rel)

    def end(self):
        p = self.p
        for rel in range(p.rings):
            index = self.base + 1 + self.right + self.left + rel
            self.w.landed(self.slot(rel, 1 - p.core), index, p.sibling)


class Scatter:
    def __init__(self, place, wires, refs, cut, pieces):
        self.p, self.w, self.cut, self.pieces = place, wires, cut, pieces
        self.own, self.away, self.near, self.out, self.into, self.stage, self.land, self.full = refs
        self.right, self.left = place.rings // 2, place.rings // 2 - 1
        self.exchange = wires.take(pieces)
        self.ring = wires.take(self.right + self.left)
        self.plane = wires.take(2 * place.lats - 1)
        self.along = wires.take(place.lats - 1)

    def put(self, part, value):
        where, _ = self.cut(part)
        first, second = value[..., 0, :, :], value[..., 1, :, :]
        mine = self.p.core == 0
        self.own[where] = jnp.where(mine, first, second)
        self.away[where] = jnp.where(mine, second, first).astype(BF16)

    def trade(self, part):
        where, index = self.cut(part)
        self.w.copy(
            self.away.at[where], self.near.at[where], self.exchange + index, self.p.sibling
        ).start()

    def traded(self, part):
        where, index = self.cut(part)
        copy = self.w.copy(
            self.away.at[where], self.near.at[where], self.exchange + index, self.p.sibling
        )
        copy.wait_send()
        copy.wait_recv()

    def share(self, rel):
        p = self.p
        z = (p.z + rel + p.rings) % p.rings
        return self.own[z] + self.near[z].astype(F32)

    def tick(self, step):
        p = self.p
        total = self.share(self.right + 1 - step)
        if step > 1:
            before = step - 2
            self.w.landed(self.into.at[before], self.ring + before, p.along_z(-1))
            total = total + self.into[before].astype(F32)
        self.out[step - 1] = total.astype(BF16)
        source = self.out.at[step - 1]
        self.w.start(
            source, self.into.at[step - 1], self.ring + step - 1, p.along_z(1), lambda: self.out.at[0]
        )
        if step <= self.left:
            slot = self.right + step - 1
            total = self.share(-(self.left + 1 - step))
            if step > 1:
                self.w.landed(self.into.at[slot - 1], self.ring + slot - 1, p.along_z(1))
                total = total + self.into[slot - 1].astype(F32)
            self.out[slot] = total.astype(BF16)
            source = self.out.at[slot]
            self.w.start(source, self.into.at[slot], self.ring + slot, p.along_z(-1), lambda: self.out.at[0])

    def spread(self, divide):
        p = self.p
        total = self.share(0)
        slots = [(self.right - 1, -1)]
        if self.left:
            slots.append((self.right + self.left - 1, 1))
        for slot, by in slots:
            self.w.landed(self.into.at[slot], self.ring + slot, p.along_z(by))
            total = total + self.into[slot].astype(F32)
        for yh in range(2):
            for sub in range(p.lats):
                self.stage[yh, sub] = divide(total[yh], sub)
        for by in range(1, 2 * p.lats):
            yh, lat = p.in_plane(by)
            self.w.start(
                self.stage.at[yh, lat],
                self.land.at[by - 1],
                self.plane + by - 1,
                p.plane_device(by),
                lambda: self.land.at[0],
            )

    def collect(self):
        p = self.p
        total = self.stage[p.yh, p.lat]
        for by in range(1, 2 * p.lats):
            self.w.landed(
                self.land.at[by - 1], self.plane + by - 1, p.plane_device(2 * p.lats - by)
            )
            total = total + self.land[by - 1]
        self.full[p.lat] = total
        block = self.full.at[p.lat]
        for by in range(1, p.lats):
            self.w.start(block, block, self.along + by - 1, p.moved(by, 0), lambda: self.full.at[0])

    def end(self):
        p = self.p
        for by in range(1, p.lats):
            lat = (p.lat - by + p.lats) % p.lats
            self.w.landed(self.full.at[lat], self.along + by - 1, (lat, p.lon))


def shifted_blocks():
    for window in range(4):
        for quarter in range(4):
            i = 2 * (window // 2) + quarter // 2
            j = 2 * (window % 2) + quarter % 2
            yield i, j, window, quarter, i == 3, j == 3


def kernel(
    lats,
    lons,
    field,
    shard_one,
    shard_two,
    shard_three,
    out_field,
    out_one,
    out_two,
    out_three,
    moved,
    back,
    x_ref,
    up_ref,
    low_up,
    hidden_one,
    packed,
    probs_ref,
    attended,
    middle,
    result,
    hidden_two,
    active,
    grad_raised,
    grad_attended,
    grad_low,
    grad_packed,
    gains,
    sums,
    one,
    two,
    three,
    *rest,
):
    scatter_refs, (send_sem, recv_sem) = rest[:-2], rest[-2:]
    p = Place(lats, lons)
    wires = Wires(send_sem, recv_sem)
    width = x_ref.shape[1]
    hid = shard_two.shape[1]
    chunk = hid // p.rings
    rows = width // lons
    tokens = 4 * TOK
    scale = (width // HEADS) ** -0.5
    per = GROUP * HEADS // width
    head = width // HEADS
    groups = width // GROUP

    barrier = pltpu.get_barrier_semaphore()
    friends = [p.plane_device(by) for by in range(1, 2 * lats)]
    friends += [p.sibling, p.along_z(1), p.along_z(-1)]
    friends += [p.moved(0, 1), p.moved(0, -1), p.moved(1, 1), p.moved(-1, -1)]
    for friend in friends:
        pl.semaphore_signal(barrier, inc=1, device_id=friend, device_id_type=MESH)
    pl.semaphore_wait(barrier, len(friends))

    def beyond(by_rows, by_columns, sign):
        return p.moved(sign * int(by_rows), sign * int(by_columns))

    halo = wires.take(7)
    edge = [item for item in shifted_blocks() if item[4] or item[5]]
    gathers = [
        Gather(p, wires, shard, whole)
        for shard, whole in ((shard_one, one), (shard_two, two), (shard_three, three))
    ]
    gathers[0].begin()
    for number, (i, j, window, quarter, down, over) in enumerate(edge):
        wires.start(
            field.at[(i + 1) % 4, (j + 1) % 4],
            moved.at[window, quarter],
            halo + number,
            beyond(down, over, -1),
            lambda: moved.at[0, 0],
        )
    gathers[0].tick(0)
    gathers[1].begin()
    gathers[2].begin()
    for step in range(1, gathers[0].right + 1):
        gathers[0].tick(step)

    for number, (i, j, window, quarter, down, over) in enumerate(edge):
        wires.landed(moved.at[window, quarter], halo + number, beyond(down, over, 1))
    for i, j, window, quarter, down, over in shifted_blocks():
        source = moved.at[window, quarter] if down or over else field.at[i + 1, j + 1]
        first = TOK * window + QUAD * quarter
        x_ref[pl.ds(first, PADQ)] = source[0].astype(F32)
        up_ref[pl.ds(first, PADQ)] = source[1].astype(F32)

    gathers[0].end()
    pending = [
        functools.partial(gather.tick, step)
        for gather in gathers[1:]
        for step in range(gather.right + 1)
    ]

    def weight(ref, first, count):
        return ref[:, :, :, :, pl.ds(first, count)].reshape(width, count)

    turned = jnp.transpose(weight(one, 4 * width, 128).astype(F32), (1, 0))
    gains[0:8] = jnp.broadcast_to(turned[0:1], (8, width))
    gains[8:16] = jnp.broadcast_to(turned[64:65], (8, width))

    def by_rows(body):
        def run(window, _):
            body(pl.ds(pl.multiple_of(window * TOK, 16), TOK))
            return 0

        lax.fori_loop(0, 4, run, 0)

    def first_norm(at):
        normed, _ = layer_norm(x_ref[at])
        hidden_one[at] = (normed * gains[0:1]).astype(BF16)
        low_up[at] = up_ref[at].astype(BF16)

    by_rows(first_norm)

    def columns(count, body):
        def run(number, _):
            body(pl.multiple_of(number * GROUP, GROUP), number)
            return 0

        lax.fori_loop(0, count, run, 0)

    def pack(first, number):
        packed[:, pl.ds(first, GROUP)] = nn(hidden_one[...], weight(one, first, GROUP)).astype(
            BF16
        )

    columns(3 * groups, pack)

    lanes = lax.broadcasted_iota(jnp.int32, (TOK, GROUP), 1) // head
    late = lax.broadcasted_iota(jnp.int32, (TOK, TOK), 0) >= TOK // 2
    late_query = lax.broadcasted_iota(jnp.int32, (TOK, TOK), 1) >= TOK // 2
    differ = late != late_query

    def head_lanes(first):
        return pl.ds(pl.multiple_of(first, GROUP), GROUP)

    def attend(number, _):
        window, group = number // groups, number % groups
        at = pl.ds(pl.multiple_of(window * TOK, 16), TOK)
        query = packed[at, head_lanes(group * GROUP)]
        keyed = packed[at, head_lanes(width + group * GROUP)]
        valued = packed[at, head_lanes(2 * width + group * GROUP)]
        split = jnp.logical_and(p.lat == lats - 1, window >= 2)
        bias = jnp.where(jnp.logical_and(differ, split), NEG, 0.0)
        value_turned = jnp.transpose(valued.astype(F32), (1, 0)).astype(BF16)
        parts = []
        for h in range(per):
            mine = jnp.where(lanes == h, keyed, jnp.zeros_like(keyed))
            scores = nt(mine, query) * scale + bias
            raised = jnp.exp(scores - jnp.max(scores, axis=0, keepdims=True))
            probs = raised * (1.0 / jnp.sum(raised, axis=0, keepdims=True))
            probs_ref[number * per + h] = probs
            parts.append(nn(value_turned[h * head : (h + 1) * head], probs.astype(BF16)))
        attended[at, head_lanes(group * GROUP)] = jnp.transpose(
            jnp.concatenate(parts, axis=0), (1, 0)
        ).astype(BF16)
        for turn, action in enumerate(pending[: 4 * groups]):
            pl.when(number == turn)(action)
        return 0

    lax.fori_loop(0, 4 * groups, attend, 0)
    for action in pending[4 * groups :]:
        action()

    def project(first, number):
        middle[:, pl.ds(first, GROUP)] = x_ref[0:tokens, pl.ds(first, GROUP)] + nn(
            attended[...], weight(one, pl.multiple_of(3 * width + first, GROUP), GROUP)
        )

    columns(groups, project)

    def second_norm(at):
        normed, _ = layer_norm(middle[at])
        hidden_two[at] = (normed * gains[8:9]).astype(BF16)

    by_rows(second_norm)
    gathers[1].end()
    gathers[2].end()

    sizes = (4 * width + 128, hid, width)
    whole_rows = (rows, rows, chunk // 4)

    def by_columns(part):
        return (slice(None), slice(None), slice(None), pl.ds(part * GROUP, GROUP)), part

    def by_hidden(part):
        first = pl.multiple_of(part * chunk, 128)
        return (slice(None), slice(None), slice(None), pl.ds(first, chunk)), part

    def whole(part):
        return (slice(None), slice(None), slice(None), slice(None)), part

    def by_ring(part):
        return (part,), part

    scatters = [
        Scatter(p, wires, scatter_refs[8 * k : 8 * k + 8], cut, pieces)
        for k, (cut, pieces) in enumerate(((whole, 1), (by_hidden, p.rings), (by_ring, p.rings)))
    ]

    def feed(number, _):
        first = pl.ds(pl.multiple_of(number * chunk, 128), chunk)
        up_weight = two[:, :, :, :, first].reshape(width, chunk)
        raised_up = nn(hidden_two[...], up_weight)
        share = 0.5 * (1.0 + lax.erf(raised_up * 0.7071067811865476))
        act = (raised_up * share).astype(BF16)
        active[:, first] = act
        slope = share + raised_up * jnp.exp(-0.5 * raised_up * raised_up) * 0.3989422804014327
        grad_down = tn(act, low_up[...])
        scatters[2].put(number, grad_down.reshape(2, 2, chunk // 4, width))
        scatters[2].trade(number)
        down_weight = three[number].reshape(chunk, width)
        grads = (nt(low_up[...], down_weight) * slope).astype(BF16)
        grad_raised[:, first] = grads
        grad_up = tn(hidden_two[...], grads)
        scatters[1].put(number, grad_up.reshape(p.rings, 2, 2, rows, chunk))
        scatters[1].trade(number)
        return 0

    lax.fori_loop(0, p.rings, feed, 0)

    def wait_trades(scatter):
        def run(number, _):
            scatter.traded(number)
            return 0

        lax.fori_loop(0, scatter.pieces, run, 0)

    wait_trades(scatters[2])
    scatters[2].tick(1)

    def lower(first, number):
        down = three[:, :, :, :, pl.ds(first, GROUP)].reshape(hid, GROUP)
        result[0:tokens, pl.ds(first, GROUP)] = middle[:, pl.ds(first, GROUP)] + nn(
            active[...], down
        )

    columns(groups, lower)

    returns = wires.take(14)

    def send_back(source, kind):
        number = 0
        for i, j, window, quarter, down, over in shifted_blocks():
            first = TOK * window + QUAD * quarter
            block = source[pl.ds(first, PADQ)].astype(BF16)
            target = out_field.at[(i + 1) % 4, (j + 1) % 4, kind]
            if down or over:
                place = back.at[number, kind]
                place[...] = block
                index = returns + 7 * kind + number
                wires.start(place, target, index, beyond(down, over, 1), lambda: back.at[0, 0])
                number += 1
            else:
                target[...] = block

    send_back(result, 0)
    wait_trades(scatters[1])
    scatters[2].tick(2)
    scatters[1].tick(1)

    def raise_back(first, number):
        share = p.rings // groups
        up_rows = two[pl.ds(number * share, share)].reshape(GROUP, hid)
        result[0:tokens, pl.ds(first, GROUP)] = nt(grad_raised[...], up_rows)

    columns(groups, raise_back)
    scatters[2].tick(3)
    scatters[1].tick(2)

    sums[...] = jnp.zeros_like(sums)

    def second_back(at):
        normed, inverse = layer_norm(middle[at])
        through, total = norm_back(result[at], normed, inverse, gains[8:9])
        sums[8:16] += jnp.broadcast_to(total, (8, width))
        grad_middle = up_ref[at] + through
        up_ref[at] = grad_middle
        grad_low[at] = grad_middle.astype(BF16)

    by_rows(second_back)
    scatters[2].tick(4)
    scatters[1].tick(3)

    def split_columns(value):
        return value.reshape(p.rings, 2, 2, rows, value.shape[1])

    def project_back(first, number):
        grad = tn(attended[...], grad_low[:, pl.ds(first, GROUP)])
        scatters[0].put_at(
            pl.ds(pl.multiple_of(3 * width + first, GROUP), GROUP), split_columns(grad)
        )
        share = p.rings // groups
        proj_rows = one[pl.ds(number * share, share), :, :, :, pl.ds(3 * width, width)]
        grad_attended[:, pl.ds(first, GROUP)] = nt(
            grad_low[...], proj_rows.reshape(GROUP, width)
        ).astype(BF16)

    columns(groups, project_back)
    scatters[2].spread(lambda total, sub: total[sub * (chunk // 4 // lats) : (sub + 1) * (chunk // 4 // lats)])
    scatters[1].tick(4)

    later = [
        scatters[2].collect,
        functools.partial(
            scatters[1].spread,
            lambda total, sub: total[:, sub * (hid // lats) : (sub + 1) * (hid // lats)],
        ),
        scatters[2].end,
        scatters[1].collect,
        scatters[1].end,
    ]

    def attend_back(number, _):
        window, group = number // groups, number % groups
        at = pl.ds(pl.multiple_of(window * TOK, 16), TOK)
        query = packed[at, head_lanes(group * GROUP)]
        keyed = packed[at, head_lanes(width + group * GROUP)]
        valued = packed[at, head_lanes(2 * width + group * GROUP)]
        upstream = grad_attended[at, head_lanes(group * GROUP)]
        key_turned = jnp.transpose(keyed.astype(F32), (1, 0)).astype(BF16)
        grad_key = jnp.zeros((TOK, GROUP), F32)
        grad_value = jnp.zeros((TOK, GROUP), F32)
        parts = []
        for h in range(per):
            probs = probs_ref[number * per + h]
            mine = lanes == h
            grad_probs = nt(jnp.where(mine, valued, jnp.zeros_like(valued)), upstream)
            grad_value = jnp.where(mine, nn(probs.astype(BF16), upstream), grad_value)
            inner = jnp.sum(grad_probs * probs, axis=0, keepdims=True)
            grad_scores = (probs * (grad_probs - inner) * scale).astype(BF16)
            grad_key = jnp.where(mine, nn(grad_scores, query), grad_key)
            parts.append(nn(key_turned[h * head : (h + 1) * head], grad_scores))
        grad_query = jnp.transpose(jnp.concatenate(parts, axis=0), (1, 0))
        grad_packed[at, head_lanes(group * GROUP)] = grad_query.astype(BF16)
        grad_packed[at, head_lanes(width + group * GROUP)] = grad_key.astype(BF16)
        grad_packed[at, head_lanes(2 * width + group * GROUP)] = grad_value.astype(BF16)
        for turn, action in enumerate(later):
            pl.when(number == turn)(action)
        return 0

    lax.fori_loop(0, 4 * groups, attend_back, 0)

    def pack_back(first, number):
        grad = tn(hidden_one[...], grad_packed[:, pl.ds(first, GROUP)])
        scatters[0].put_at(pl.ds(first, GROUP), split_columns(grad))

    columns(3 * groups, pack_back)

    def unpack(first, number):
        share = p.rings // groups
        rows_here = one[pl.ds(number * share, share), :, :, :, pl.ds(0, 3 * width)]
        result[0:tokens, pl.ds(first, GROUP)] = nt(
            grad_packed[...], rows_here.reshape(GROUP, 3 * width)
        )

    columns(groups, unpack)

    def first_back(at):
        normed, inverse = layer_norm(x_ref[at])
        through, total = norm_back(result[at], normed, inverse, gains[0:1])
        sums[0:8] += jnp.broadcast_to(total, (8, width))
        up_ref[at] = up_ref[at] + through

    by_rows(first_back)
    line = lax.broadcasted_iota(jnp.int32, (128, width), 0)
    both = jnp.where(line < 64, sums[0:1], sums[8:9])
    scatters[0].put_at(pl.ds(4 * width, 128), split_columns(jnp.transpose(both, (1, 0))))
    scatters[0].trade(0)
    send_back(up_ref, 1)
    scatters[0].traded(0)
    for step in range(1, scatters[0].right + 1):
        scatters[0].tick(step)
    share = 4 * width // lats
    scatters[0].spread(
        lambda total, sub: jnp.concatenate(
            [total[:, sub * share : (sub + 1) * share], total[:, 4 * width :]], axis=1
        )
    )
    scatters[0].collect()
    scatters[0].end()
    for sub in range(lats):
        out_three[sub * (chunk // 4 // lats) : (sub + 1) * (chunk // 4 // lats)] = scatters[2].full[
            sub
        ]
        out_two[:, sub * (hid // lats) : (sub + 1) * (hid // lats)] = scatters[1].full[sub]
        out_one[:, sub * share : (sub + 1) * share] = scatters[0].full[sub, :, 0:share]
    out_one[:, 4 * width :] = scatters[0].full[0, :, share:]
    number = 0
    for i, j, window, quarter, down, over in shifted_blocks():
        if down or over:
            for kind in range(2):
                wires.landed(
                    out_field.at[(i + 1) % 4, (j + 1) % 4, kind],
                    returns + 7 * kind + number,
                    beyond(down, over, -1),
                )
            number += 1
    wires.finish(p.sibling)


def put_at(self, columns, value):
    first, second = value[..., 0, :, :], value[..., 1, :, :]
    mine = self.p.core == 0
    self.own[:, :, :, columns] = jnp.where(mine, first, second)
    self.away[:, :, :, columns] = jnp.where(mine, second, first).astype(BF16)


Scatter.put_at = put_at


def blocks_of(field):
    height, breadth, depth = field.shape
    shaped = field.reshape(height // SHIFT, SHIFT, breadth // SHIFT, SHIFT, depth)
    shaped = shaped.transpose(0, 2, 1, 3, 4).reshape(4, 4, QUAD, depth)
    return jnp.pad(shaped, ((0, 0), (0, 0), (0, PADQ - QUAD), (0, 0)))


def field_of(blocks):
    depth = blocks.shape[-1]
    shaped = blocks[:, :, :QUAD].reshape(4, 4, SHIFT, SHIFT, depth)
    return shaped.transpose(0, 2, 1, 3, 4).reshape(4 * SHIFT, 4 * SHIFT, depth)


def body(
    lats,
    lons,
    cells,
    cotangent,
    land,
    land_embed,
    qkv_weight,
    proj_weight,
    up_weight,
    down_weight,
    gain_one,
    gain_two,
):
    start = (
        cells.astype(F32) + land[:, :, None].astype(F32) * land_embed[None, None, :]
    ).astype(BF16)
    field = jnp.stack([blocks_of(start), blocks_of(cotangent)], axis=2)
    rows, hid = up_weight.shape
    width = cells.shape[2]
    deep = down_weight.shape[0]
    tokens = 4 * TOK
    rings = lons // 4
    shard_one = jnp.concatenate(
        [
            qkv_weight,
            proj_weight,
            jnp.broadcast_to(gain_one[:, None], (rows, 64)),
            jnp.broadcast_to(gain_two[:, None], (rows, 64)),
        ],
        axis=1,
    )
    wide = 4 * width + 128

    def scatter_scratch(lines, across, piece):
        return [
            pltpu.VMEM((rings, 2, lines, across), F32),
            pltpu.VMEM((rings, 2, lines, across), BF16),
            pltpu.VMEM((rings, 2, lines, across), BF16),
            pltpu.VMEM((rings - 1, 2, lines, across), BF16),
            pltpu.VMEM((rings - 1, 2, lines, across), BF16),
            pltpu.VMEM((2, lats) + piece, F32),
            pltpu.VMEM((2 * lats - 1,) + piece, F32),
            pltpu.VMEM((lats,) + piece, F32),
        ]

    scratch = [
        pltpu.VMEM((4, 4, 2, PADQ, width), BF16),
        pltpu.VMEM((7, 2, PADQ, width), BF16),
        pltpu.VMEM((tokens + 16, width), F32),
        pltpu.VMEM((tokens + 16, width), F32),
        pltpu.VMEM((tokens, width), BF16),
        pltpu.VMEM((tokens, width), BF16),
        pltpu.VMEM((tokens, 3 * width), BF16),
        pltpu.VMEM((4 * HEADS, TOK, TOK), F32),
        pltpu.VMEM((tokens, width), BF16),
        pltpu.VMEM((tokens, width), F32),
        pltpu.VMEM((tokens + 16, width), F32),
        pltpu.VMEM((tokens, width), BF16),
        pltpu.VMEM((tokens, hid), BF16),
        pltpu.VMEM((tokens, hid), BF16),
        pltpu.VMEM((tokens, width), BF16),
        pltpu.VMEM((tokens, width), BF16),
        pltpu.VMEM((tokens, 3 * width), BF16),
        pltpu.VMEM((16, width), F32),
        pltpu.VMEM((16, width), F32),
        pltpu.VMEM((rings, 2, 2, rows, wide), BF16),
        pltpu.VMEM((rings, 2, 2, rows, hid), BF16),
        pltpu.VMEM((rings, 2, 2, deep, width), BF16),
    ]
    scratch += scatter_scratch(rows, wide, (rows, 4 * width // lats + 128))
    scratch += scatter_scratch(rows, hid, (rows, hid // lats))
    scratch += scatter_scratch(deep, width, (deep // lats, width))
    wires = 7 + 14 + 3 * (2 * rings)
    wires += (1 + rings - 1 + 3 * lats - 2) + 2 * (rings + rings - 1 + 3 * lats - 2)
    scratch += [pltpu.SemaphoreType.DMA((wires,)), pltpu.SemaphoreType.DMA((wires,))]
    vmem = pl.BlockSpec(memory_space=pltpu.VMEM)
    out_field, one, two, three = pl.pallas_call(
        functools.partial(kernel, lats, lons),
        out_shape=(
            jax.ShapeDtypeStruct((4, 4, 2, PADQ, width), BF16),
            jax.ShapeDtypeStruct((rows, wide), F32),
            jax.ShapeDtypeStruct((rows, hid), F32),
            jax.ShapeDtypeStruct((deep, width), F32),
        ),
        in_specs=[vmem] * 4,
        out_specs=(vmem,) * 4,
        scratch_shapes=scratch,
        compiler_params=pltpu.CompilerParams(
            collective_id=0, has_side_effects=True, vmem_limit_bytes=63 * 2**20
        ),
        name="block",
    )(field, shard_one, up_weight, down_weight)
    return (
        field_of(out_field[:, :, 0]),
        field_of(out_field[:, :, 1]),
        one[:, : 3 * width],
        one[:, 3 * width : 4 * width],
        two,
        three,
        one[:, 4 * width],
        one[:, 4 * width + 64],
    )


def solution(mesh):
    placed = (
        P("lat", "lon", None),
        P("lat", "lon", None),
        P("lat", "lon"),
        P(),
        P("lon", None),
        P("lon", None),
        P("lon", None),
        P("lon", None),
        P("lon"),
        P("lon"),
    )
    return jax.shard_map(
        functools.partial(body, mesh.shape["lat"], mesh.shape["lon"]),
        mesh=mesh,
        in_specs=placed,
        out_specs=(
            P("lat", "lon", None),
            P("lat", "lon", None),
            P("lon", None),
            P("lon", None),
            P("lon", None),
            P("lon", None),
            P("lon"),
            P("lon"),
        ),
        check_vma=False,
    )
```

time: 925 us -> 206 us (0.22)
  waiting for transfers between devices: 518 us -> 0 us
  blocking collectives: 198 us -> 0 us
  Pallas kernels: 0 us -> 187 us
  matrix products: 112 us -> 0 us
  local copies, waits for them, and re-layouts: 48.3 us -> 13.3 us
  between operations: 16.2 us -> 0.79 us
  starting transfers between devices: 12.8 us -> 0 us
  other arithmetic: 14.7 us -> 3.3 us
    reduce_scatter x4 -> x0, waiting for transfers between devices: 403 us -> none  [the longest x1 130 us: body(): lax.psum_scatter(grads[2], 'lon', scatter_dimension=0, tiled=True)]
    pallas_call x0 -> x1, Pallas kernels: none -> 187 us  [body(): pl.pallas_call(functools.partial(kernel, lats, lons), out_shape=(jax.Shap...]
    unnamed x2 -> x0, blocking collectives: 117 us -> none
    dot_general x17 -> x0, matrix products: 103 us -> none  [the longest x5 48.5 us: float_einsum(): return jnp.einsum(form, left, right, preferred_element_type=jnp.float32)]
    all_gather x3 -> x0, waiting for transfers between devices: 59.5 us -> none  [the longest x1 59.5 us: body(): lax.all_gather(down_weight, 'lon', axis=0, tiled=True)]
    psum x1 -> x0, waiting for transfers between devices: 47.2 us -> none  [body(): lax.psum((shares[0], shares[1], shares[2], shares[3], shares[4], shares[5...]
    all_gather x1 -> x0, blocking collectives: 46.7 us -> none  [body(): lax.all_gather(proj_weight, 'lon', axis=0, tiled=True)]
    psum x1 -> x0, blocking collectives: 34.2 us -> none  [body(): lax.psum((shares[0], shares[1], shares[2], shares[3], shares[4], shares[5...]
  transfers between devices with their start and end apart: 16 -> 0, of which waited for: 8 -> 0; matrix products, arithmetic and copies ran while one was open for 10% -> 0% of each run, Pallas kernels for 0% -> 0%
where the time goes in v1:
time: 206 us; the launch traced here: 205 us
  Pallas kernels  187 us (91%)
  local copies, waits for them, and re-layouts  13.3 us (6%)
  other arithmetic  3.3 us (2%)
    pallas_call x1, Pallas kernels, body(): pl.pallas_call(functools.partial(kernel, lats, lons), out_shape=(jax.Shap...  187 us

profile of v1, /device:TPU:32, one launch (start us, length us, event | category | flops | bytes accessed | tf_op | source)
XLA Modules:
  0.0 204.6 jit_solution(14292327727741643184)
XLA Ops:
  0.6 0.7 broadcast_in_dim.4
  1.4 0.7 broadcast_in_dim.5
  2.1 0.7 convert_element_type.14
  2.8 1.5 concatenate.3.shard_one
  4.3 1.3 add_convert_fusion
  5.6 0.2 reshape.45
  5.8 0.0 copy-start
  5.8 0.3 copy.22
  6.1 0.1 copy.23
  6.2 0.6 copy-done
  6.9 0.2 reshape.47
  7.1 0.3 copy.24
  7.4 0.1 copy.25
  7.5 0.2 pad_bitcast_fusion
  7.7 1.3 pad_maximum_fusion.field
  9.0 187.2 %block.1 = (bf16[4,4,2,48,512]{4,3,2,1,0:T(8,128)(2,1)}, f32[16,2176]{1,0:T(8,128)}, f32[16,2048]{1,0:T(8,128)}, f32[64,512]{1,0:T(8,128)}) custom-call(bf16[4,4,2,48,512]{4,3,2,1,0:T(8,128)(2,1)} %pad_maximum_fusion.field, bf16[16,2176]{1,0:T(8,128)(2,1)} %concatenate.3.shard_one, bf16[16,2048]{1,0:T(8,128)(2,1)} %shard_two.1, bf16[64,512]{1,0:T(8,128)(2,1)} %shard_three.1), custom_call_target="tpu_custom_call" | custom-call | tf_op jit(solution)/shard_map/block/pallas_call | solution.py:780
  196.2 1.5 slice_bitcast_fusion
  197.7 0.0 copy-start.1
  197.8 0.3 copy.28
  198.1 0.5 copy-done.1
  198.6 0.7 slice_reduce_fusion
  199.3 0.6 slice.29
  199.9 0.6 slice.28
  200.6 0.2 copy.29
  200.7 1.0 reshape.52
  201.8 0.3 copy.26
  202.1 0.0 copy-start.3
  202.1 0.0 copy-start.2
  202.1 0.2 copy.27
  202.3 1.0 reshape.50
  203.3 0.0 copy-done.3
  203.3 0.7 copy.32
  204.0 0.0 copy-done.2
  204.0 0.7 copy.33
  (2 shorter events, 0.1 us)
Async XLA Ops:
  5.8 1.1 copy-start
  197.7 0.9 copy-start.1
  202.1 1.2 copy-start.3
  202.1 1.8 copy-start.2

commit v2 on v1

--- a/solution.py
+++ b/solution.py
@@ -50,6 +50,19 @@
     return inner * inverse, jnp.sum(upstream * normed, axis=0, keepdims=True)
 
 
+class Marks:
+    def __init__(self):
+        self.open = None
+
+    def __call__(self, name=None):
+        if self.open is not None:
+            self.open.__exit__(None, None, None)
+        self.open = None
+        if name is not None:
+            self.open = jax.named_scope(name)
+            self.open.__enter__()
+
+
 class Place:
     def __init__(self, lats, lons):
         self.lats, self.lons, self.rings = lats, lons, lons // 4
@@ -116,126 +129,150 @@
 class Gather:
     def __init__(self, place, wires, shard, whole):
         self.p, self.w, self.shard, self.whole = place, wires, shard, whole
-        self.right, self.left = place.rings // 2, place.rings // 2 - 1
-        self.base = wires.take(1 + self.right + self.left + place.rings)
-
-    def slot(self, rel, core):
+        self.half = place.rings // 2
+        self.last = 2 * self.half
+        self.far = wires.take(1)
+        self.way = {1: wires.take(self.last - 1), -1: wires.take(self.last - 1)}
+        self.side = wires.take(place.rings)
+
+    def slot(self, rel, other):
+        p = self.p
+        yh = 1 - p.yh if other else p.yh
+        return self.whole.at[(p.z - rel + p.rings) % p.rings, yh, p.core]
+
+    def pair(self, rel, core):
         p = self.p
         return self.whole.at[(p.z - rel + p.rings) % p.rings, :, core]
 
-    def begin(self):
-        p = self.p
-        here = self.whole.at[p.z, p.yh, p.core]
-        here[...] = self.shard[...]
-        self.w.start(self.shard, here, self.base, p.partner, lambda: self.shard)
+    def forward(self, way, hop, other):
+        if hop == self.half - 1 and other != (way < 0):
+            return
+        index = self.way[way] + (2 * hop + other if hop < self.half - 1 else 2 * hop)
+        block = self.slot(way * hop, other)
+        self.w.start(block, block, index, self.p.along_z(way), lambda: self.whole.at[0, 0, 0])
+
+    def landed(self, way, hop, other):
+        index = self.way[way] + (2 * (hop - 1) + other if hop < self.half else 2 * (hop - 1))
+        self.w.landed(self.slot(way * hop, other), index, self.p.along_z(-way))
 
     def share(self, rel):
         p = self.p
-        index = self.base + 1 + self.right + self.left + rel
-        block = self.slot(rel, p.core)
+        index = self.side + rel % p.rings
+        block = self.pair(rel, p.core)
         self.w.start(block, block, index, p.sibling, lambda: self.whole.at[0, :, 0])
 
     def tick(self, step):
         p = self.p
         if step == 0:
-            self.w.landed(self.whole.at[p.z, 1 - p.yh, p.core], self.base, p.partner)
-            arrived = (0,)
+            here = self.slot(0, 0)
+            here[...] = self.shard[...]
+            for way in (1, -1):
+                self.forward(way, 0, 0)
+            self.w.start(self.shard, here, self.far, p.partner, lambda: self.shard)
+        elif step == 1:
+            self.w.landed(self.slot(0, 1), self.far, p.partner)
+            for way in (1, -1):
+                self.forward(way, 0, 1)
+            self.share(0)
+        elif step < self.last:
+            hop, other = step // 2, step % 2
+            for way in (1, -1):
+                self.landed(way, hop, other)
+                self.forward(way, hop, other)
+            if other:
+                for way in (1, -1):
+                    self.share(way * hop)
         else:
-            arrived = []
-            self.w.landed(self.slot(step, p.core), self.base + step, p.along_z(-1))
-            arrived.append(step)
-            if step <= self.left:
-                index = self.base + self.right + step
-                self.w.landed(self.slot(p.rings - step, p.core), index, p.along_z(1))
-                arrived.append(p.rings - step)
-        if step < self.right:
-            block = self.slot(step, p.core)
-            index = self.base + 1 + step
-            self.w.start(block, block, index, p.along_z(1), lambda: self.whole.at[0, :, 0])
-        if step < self.left:
-            block = self.slot((p.rings - step) % p.rings, p.core)
-            index = self.base + 1 + self.right + step
-            self.w.start(block, block, index, p.along_z(-1), lambda: self.whole.at[0, :, 0])
-        for rel in arrived:
-            self.share(rel)
+            self.landed(1, self.half, 0)
+            self.landed(-1, self.half, 1)
+            self.share(self.half)
 
     def end(self):
         p = self.p
         for rel in range(p.rings):
-            index = self.base + 1 + self.right + self.left + rel
-            self.w.landed(self.slot(rel, 1 - p.core), index, p.sibling)
+            self.w.landed(self.pair(rel, 1 - p.core), self.side + rel, p.sibling)
 
 
 class Scatter:
-    def __init__(self, place, wires, refs, cut, pieces):
-        self.p, self.w, self.cut, self.pieces = place, wires, cut, pieces
+    def __init__(self, place, wires, refs, pieces):
+        self.p, self.w, self.pieces = place, wires, pieces
         self.own, self.away, self.near, self.out, self.into, self.stage, self.land, self.full = refs
-        self.right, self.left = place.rings // 2, place.rings // 2 - 1
+        self.half = place.rings // 2
+        self.last = 2 * self.half - 1
         self.exchange = wires.take(pieces)
-        self.ring = wires.take(self.right + self.left)
+        self.ring = wires.take(2 * self.last)
         self.plane = wires.take(2 * place.lats - 1)
         self.along = wires.take(place.lats - 1)
-
-    def put(self, part, value):
-        where, _ = self.cut(part)
+        self.lines = self.own.shape[2] // place.lats
+
+    def put(self, where, value):
         first, second = value[..., 0, :, :], value[..., 1, :, :]
         mine = self.p.core == 0
         self.own[where] = jnp.where(mine, first, second)
         self.away[where] = jnp.where(mine, second, first).astype(BF16)
 
-    def trade(self, part):
-        where, index = self.cut(part)
+    def trade(self, where, index):
         self.w.copy(
             self.away.at[where], self.near.at[where], self.exchange + index, self.p.sibling
         ).start()
 
-    def traded(self, part):
-        where, index = self.cut(part)
+    def traded(self, where, index):
         copy = self.w.copy(
             self.away.at[where], self.near.at[where], self.exchange + index, self.p.sibling
         )
         copy.wait_send()
         copy.wait_recv()
 
-    def share(self, rel):
+    def share(self, rel, yh):
         p = self.p
         z = (p.z + rel + p.rings) % p.rings
-        return self.own[z] + self.near[z].astype(F32)
+        return self.own[z, yh] + self.near[z, yh].astype(F32)
+
+    def pass_on(self, way, rel, yh):
+        p = self.p
+        base = 0 if way > 0 else self.last
+        slot = base + 2 * rel - 2 + yh if rel < self.half else base + self.last - 1
+        total = self.share(way * rel, yh)
+        longest = self.half if (yh == 0) == (way > 0) else self.half - 1
+        if rel < longest:
+            before = base + 2 * rel + yh if rel + 1 < self.half else base + self.last - 1
+            self.w.landed(self.into.at[before], self.ring + before, p.along_z(-way))
+            total = total + self.into[before].astype(F32)
+        self.out[slot] = total.astype(BF16)
+        self.w.start(
+            self.out.at[slot],
+            self.into.at[slot],
+            self.ring + slot,
+            p.along_z(way),
+            lambda: self.out.at[0],
+        )
 
     def tick(self, step):
+        if step == 0:
+            self.pass_on(1, self.half, 0)
+            self.pass_on(-1, self.half, 1)
+            self.pass_on(1, self.half - 1, 1)
+            self.pass_on(-1, self.half - 1, 0)
+        else:
+            rel = self.half - (step + 1) // 2
+            first = step % 2
+            if not first:
+                rel -= 1
+            if rel < 1:
+                return
+            self.pass_on(1, rel, 0 if first else 1)
+            self.pass_on(-1, rel, 1 if first else 0)
+
+    def spread(self):
         p = self.p
-        total = self.share(self.right + 1 - step)
-        if step > 1:
-            before = step - 2
-            self.w.landed(self.into.at[before], self.ring + before, p.along_z(-1))
-            total = total + self.into[before].astype(F32)
-        self.out[step - 1] = total.astype(BF16)
-        source = self.out.at[step - 1]
-        self.w.start(
-            source, self.into.at[step - 1], self.ring + step - 1, p.along_z(1), lambda: self.out.at[0]
-        )
-        if step <= self.left:
-            slot = self.right + step - 1
-            total = self.share(-(self.left + 1 - step))
-            if step > 1:
-                self.w.landed(self.into.at[slot - 1], self.ring + slot - 1, p.along_z(1))
-                total = total + self.into[slot - 1].astype(F32)
-            self.out[slot] = total.astype(BF16)
-            source = self.out.at[slot]
-            self.w.start(source, self.into.at[slot], self.ring + slot, p.along_z(-1), lambda: self.out.at[0])
-
-    def spread(self, divide):
-        p = self.p
-        total = self.share(0)
-        slots = [(self.right - 1, -1)]
-        if self.left:
-            slots.append((self.right + self.left - 1, 1))
-        for slot, by in slots:
-            self.w.landed(self.into.at[slot], self.ring + slot, p.along_z(by))
-            total = total + self.into[slot].astype(F32)
         for yh in range(2):
+            total = self.share(0, yh)
+            for way in (1, -1):
+                slot = yh if way > 0 else self.last + yh
+                self.w.landed(self.into.at[slot], self.ring + slot, p.along_z(-way))
+                total = total + self.into[slot].astype(F32)
             for sub in range(p.lats):
-                self.stage[yh, sub] = divide(total[yh], sub)
+                self.stage[yh, sub] = total[sub * self.lines : (sub + 1) * self.lines]
         for by in range(1, 2 * p.lats):
             yh, lat = p.in_plane(by)
             self.w.start(
@@ -257,13 +294,19 @@
         self.full[p.lat] = total
         block = self.full.at[p.lat]
         for by in range(1, p.lats):
-            self.w.start(block, block, self.along + by - 1, p.moved(by, 0), lambda: self.full.at[0])
+            self.w.start(
+                block, block, self.along + by - 1, p.moved(by, 0), lambda: self.full.at[0]
+            )
 
     def end(self):
         p = self.p
         for by in range(1, p.lats):
             lat = (p.lat - by + p.lats) % p.lats
             self.w.landed(self.full.at[lat], self.along + by - 1, (lat, p.lon))
+
+    def write(self, store):
+        for sub in range(self.p.lats):
+            store(slice(sub * self.lines, (sub + 1) * self.lines), self.full[sub])
 
 
 def shifted_blocks():
@@ -322,6 +365,8 @@
     head = width // HEADS
     groups = width // GROUP
 
+    mark = Marks()
+    mark("barrier")
     barrier = pltpu.get_barrier_semaphore()
     friends = [p.plane_device(by) for by in range(1, 2 * lats)]
     friends += [p.sibling, p.along_z(1), p.along_z(-1)]
@@ -333,45 +378,62 @@
     def beyond(by_rows, by_columns, sign):
         return p.moved(sign * int(by_rows), sign * int(by_columns))
 
-    halo = wires.take(7)
+    mark("gather_one")
+    halo = wires.take(14)
     edge = [item for item in shifted_blocks() if item[4] or item[5]]
-    gathers = [
+    first_weight, second_weight, third_weight = [
         Gather(p, wires, shard, whole)
         for shard, whole in ((shard_one, one), (shard_two, two), (shard_three, three))
     ]
-    gathers[0].begin()
-    for number, (i, j, window, quarter, down, over) in enumerate(edge):
-        wires.start(
-            field.at[(i + 1) % 4, (j + 1) % 4],
-            moved.at[window, quarter],
-            halo + number,
-            beyond(down, over, -1),
-            lambda: moved.at[0, 0],
-        )
-    gathers[0].tick(0)
-    gathers[1].begin()
-    gathers[2].begin()
-    for step in range(1, gathers[0].right + 1):
-        gathers[0].tick(step)
-
-    for number, (i, j, window, quarter, down, over) in enumerate(edge):
-        wires.landed(moved.at[window, quarter], halo + number, beyond(down, over, 1))
-    for i, j, window, quarter, down, over in shifted_blocks():
-        source = moved.at[window, quarter] if down or over else field.at[i + 1, j + 1]
-        first = TOK * window + QUAD * quarter
-        x_ref[pl.ds(first, PADQ)] = source[0].astype(F32)
-        up_ref[pl.ds(first, PADQ)] = source[1].astype(F32)
-
-    gathers[0].end()
-    pending = [
-        functools.partial(gather.tick, step)
-        for gather in gathers[1:]
-        for step in range(gather.right + 1)
-    ]
+
+    def send_halo(kind):
+        for number, (i, j, window, quarter, down, over) in enumerate(edge):
+            wires.start(
+                field.at[(i + 1) % 4, (j + 1) % 4, kind],
+                moved.at[window, quarter, kind],
+                halo + 7 * kind + number,
+                beyond(down, over, -1),
+                lambda: moved.at[0, 0, 0],
+            )
+
+    def assemble(kind, windows, target):
+        numbers = {item[2:4]: number for number, item in enumerate(edge)}
+        for i, j, window, quarter, down, over in shifted_blocks():
+            if window not in windows:
+                continue
+            if down or over:
+                wires.landed(
+                    moved.at[window, quarter, kind],
+                    halo + 7 * kind + numbers[(window, quarter)],
+                    beyond(down, over, 1),
+                )
+                block = moved[window, quarter, kind]
+            else:
+                block = field[i + 1, j + 1, kind]
+            target[pl.ds(TOK * window + QUAD * quarter, PADQ)] = block.astype(F32)
+
+    first_weight.tick(0)
+    send_halo(0)
+    first_weight.tick(1)
+    assemble(0, (0,), x_ref)
+    first_weight.tick(2)
+    first_weight.tick(3)
+    assemble(0, (1, 2), x_ref)
+    first_weight.tick(4)
+    first_weight.tick(5)
+    assemble(0, (3,), x_ref)
+    for step in range(6, first_weight.last + 1):
+        first_weight.tick(step)
+    second_weight.tick(0)
+    send_halo(1)
+    second_weight.tick(1)
+    mark("gather_one_end")
+    first_weight.end()
 
     def weight(ref, first, count):
         return ref[:, :, :, :, pl.ds(first, count)].reshape(width, count)
 
+    mark("norm_one")
     turned = jnp.transpose(weight(one, 4 * width, 128).astype(F32), (1, 0))
     gains[0:8] = jnp.broadcast_to(turned[0:1], (8, width))
     gains[8:16] = jnp.broadcast_to(turned[64:65], (8, width))
@@ -386,7 +448,6 @@
     def first_norm(at):
         normed, _ = layer_norm(x_ref[at])
         hidden_one[at] = (normed * gains[0:1]).astype(BF16)
-        low_up[at] = up_ref[at].astype(BF16)
 
     by_rows(first_norm)
 
@@ -402,8 +463,10 @@
             BF16
         )
 
+    mark("qkv")
     columns(3 * groups, pack)
 
+    mark("attend")
     lanes = lax.broadcasted_iota(jnp.int32, (TOK, GROUP), 1) // head
     late = lax.broadcasted_iota(jnp.int32, (TOK, TOK), 0) >= TOK // 2
     late_query = lax.broadcasted_iota(jnp.int32, (TOK, TOK), 1) >= TOK // 2
@@ -411,6 +474,23 @@
 
     def head_lanes(first):
         return pl.ds(pl.multiple_of(first, GROUP), GROUP)
+
+    def at_turn(number, turns, turn_of):
+        for turn in range(turn_of, len(turns), 2):
+            if turns[turn]:
+
+                def act(turn=turn):
+                    for action in turns[turn]:
+                        action()
+
+                pl.when(number == turn // 2)(act)
+
+    turns = [[] for _ in range(8 * groups)]
+    for step in range(2, second_weight.last + 1):
+        turns[2 * step - 3].append(functools.partial(second_weight.tick, step))
+    turns[11].append(functools.partial(third_weight.tick, 0))
+    turns[13].append(functools.partial(third_weight.tick, 1))
+    turns[15].append(functools.partial(third_weight.tick, 2))
 
     def attend(number, _):
         window, group = number // groups, number % groups
@@ -423,6 +503,8 @@
         value_turned = jnp.transpose(valued.astype(F32), (1, 0)).astype(BF16)
         parts = []
         for h in range(per):
+            if h == per // 2:
+                at_turn(number, turns, 0)
             mine = jnp.where(lanes == h, keyed, jnp.zeros_like(keyed))
             scores = nt(mine, query) * scale + bias
             raised = jnp.exp(scores - jnp.max(scores, axis=0, keepdims=True))
@@ -432,13 +514,12 @@
         attended[at, head_lanes(group * GROUP)] = jnp.transpose(
             jnp.concatenate(parts, axis=0), (1, 0)
         ).astype(BF16)
-        for turn, action in enumerate(pending[: 4 * groups]):
-            pl.when(number == turn)(action)
+        at_turn(number, turns, 1)
         return 0
 
     lax.fori_loop(0, 4 * groups, attend, 0)
-    for action in pending[4 * groups :]:
-        action()
+    mark("project")
+    third_weight.tick(3)
 
     def project(first, number):
         middle[:, pl.ds(first, GROUP)] = x_ref[0:tokens, pl.ds(first, GROUP)] + nn(
@@ -446,38 +527,53 @@
         )
 
     columns(groups, project)
+    third_weight.tick(4)
+    assemble(1, (0, 1, 2, 3), up_ref)
+    third_weight.tick(5)
 
     def second_norm(at):
         normed, _ = layer_norm(middle[at])
         hidden_two[at] = (normed * gains[8:9]).astype(BF16)
+        low_up[at] = up_ref[at].astype(BF16)
 
     by_rows(second_norm)
-    gathers[1].end()
-    gathers[2].end()
-
-    sizes = (4 * width + 128, hid, width)
-    whole_rows = (rows, rows, chunk // 4)
-
-    def by_columns(part):
-        return (slice(None), slice(None), slice(None), pl.ds(part * GROUP, GROUP)), part
-
-    def by_hidden(part):
-        first = pl.multiple_of(part * chunk, 128)
-        return (slice(None), slice(None), slice(None), pl.ds(first, chunk)), part
-
-    def whole(part):
-        return (slice(None), slice(None), slice(None), slice(None)), part
-
-    def by_ring(part):
-        return (part,), part
-
-    scatters = [
-        Scatter(p, wires, scatter_refs[8 * k : 8 * k + 8], cut, pieces)
-        for k, (cut, pieces) in enumerate(((whole, 1), (by_hidden, p.rings), (by_ring, p.rings)))
+    mark("gather_end")
+    for step in range(6, third_weight.last + 1):
+        third_weight.tick(step)
+    second_weight.end()
+    third_weight.end()
+
+    scatter_down = Scatter(p, wires, scatter_refs[0:8], p.rings)
+    scatter_up = Scatter(p, wires, scatter_refs[8:16], p.rings + 1)
+    scatter_packed = [
+        Scatter(p, wires, scatter_refs[16 + 8 * k : 24 + 8 * k], 1) for k in range(groups)
     ]
+    every = slice(None)
+
+    def across(first, count):
+        return (every, every, every, pl.ds(first, count))
+
+    def ring_place(rel):
+        return (p.z + rel + p.rings) % p.rings
+
+    def down_tick(step):
+        if step % 2 == 0:
+            needed = (p.rings // 2,) if step == 0 else ()
+            near = p.rings // 2 - 1 - step // 2
+            for rel in needed + (near, -near):
+                place = ring_place(rel)
+                scatter_down.traded((place,), place)
+        scatter_down.tick(step)
+
+    steps = p.rings - 2
+    turns_feed = ((max(2, p.rings // 2 - 1), 0), (p.rings - 2, 1), (p.rings - 1, 2))
 
     def feed(number, _):
-        first = pl.ds(pl.multiple_of(number * chunk, 128), chunk)
+        rel = jnp.where(
+            number % 2 == 1, p.rings // 2 - (number + 1) // 2, p.rings // 2 + number // 2
+        )
+        place = ring_place(rel)
+        first = pl.ds(pl.multiple_of(place * chunk, 128), chunk)
         up_weight = two[:, :, :, :, first].reshape(width, chunk)
         raised_up = nn(hidden_two[...], up_weight)
         share = 0.5 * (1.0 + lax.erf(raised_up * 0.7071067811865476))
@@ -485,27 +581,22 @@
         active[:, first] = act
         slope = share + raised_up * jnp.exp(-0.5 * raised_up * raised_up) * 0.3989422804014327
         grad_down = tn(act, low_up[...])
-        scatters[2].put(number, grad_down.reshape(2, 2, chunk // 4, width))
-        scatters[2].trade(number)
-        down_weight = three[number].reshape(chunk, width)
+        scatter_down.put((place,), grad_down.reshape(2, 2, chunk // 4, width))
+        scatter_down.trade((place,), place)
+        down_weight = three[place].reshape(chunk, width)
         grads = (nt(low_up[...], down_weight) * slope).astype(BF16)
         grad_raised[:, first] = grads
         grad_up = tn(hidden_two[...], grads)
-        scatters[1].put(number, grad_up.reshape(p.rings, 2, 2, rows, chunk))
-        scatters[1].trade(number)
+        where = across(pl.multiple_of(place * chunk, 128), chunk)
+        scatter_up.put(where, grad_up.reshape(p.rings, 2, 2, rows, chunk))
+        scatter_up.trade(where, place)
+        for turn, step in turns_feed:
+            if step < steps:
+                pl.when(number == turn)(functools.partial(down_tick, step))
         return 0
 
+    mark("feed")
     lax.fori_loop(0, p.rings, feed, 0)
-
-    def wait_trades(scatter):
-        def run(number, _):
-            scatter.traded(number)
-            return 0
-
-        lax.fori_loop(0, scatter.pieces, run, 0)
-
-    wait_trades(scatters[2])
-    scatters[2].tick(1)
 
     def lower(first, number):
         down = three[:, :, :, :, pl.ds(first, GROUP)].reshape(hid, GROUP)
@@ -513,7 +604,10 @@
             active[...], down
         )
 
+    mark("lower")
     columns(groups, lower)
+    for step in range(3, min(steps, 4)):
+        down_tick(step)
 
     returns = wires.take(14)
 
@@ -532,19 +626,20 @@
             else:
                 target[...] = block
 
+    mark("return_out")
     send_back(result, 0)
-    wait_trades(scatters[1])
-    scatters[2].tick(2)
-    scatters[1].tick(1)
+    for step in range(4, min(steps, 5)):
+        down_tick(step)
 
     def raise_back(first, number):
         share = p.rings // groups
         up_rows = two[pl.ds(number * share, share)].reshape(GROUP, hid)
         result[0:tokens, pl.ds(first, GROUP)] = nt(grad_raised[...], up_rows)
 
+    mark("raise_back")
     columns(groups, raise_back)
-    scatters[2].tick(3)
-    scatters[1].tick(2)
+    for step in range(5, steps):
+        down_tick(step)
 
     sums[...] = jnp.zeros_like(sums)
 
@@ -556,41 +651,39 @@
         up_ref[at] = grad_middle
         grad_low[at] = grad_middle.astype(BF16)
 
+    mark("norm_two_back")
     by_rows(second_back)
-    scatters[2].tick(4)
-    scatters[1].tick(3)
 
     def split_columns(value):
         return value.reshape(p.rings, 2, 2, rows, value.shape[1])
 
     def project_back(first, number):
         grad = tn(attended[...], grad_low[:, pl.ds(first, GROUP)])
-        scatters[0].put_at(
-            pl.ds(pl.multiple_of(3 * width + first, GROUP), GROUP), split_columns(grad)
-        )
+        scatter_up.put(across(pl.multiple_of(hid + first, GROUP), GROUP), split_columns(grad))
         share = p.rings // groups
         proj_rows = one[pl.ds(number * share, share), :, :, :, pl.ds(3 * width, width)]
         grad_attended[:, pl.ds(first, GROUP)] = nt(
             grad_low[...], proj_rows.reshape(GROUP, width)
         ).astype(BF16)
 
+    mark("project_back")
     columns(groups, project_back)
-    scatters[2].spread(lambda total, sub: total[sub * (chunk // 4 // lats) : (sub + 1) * (chunk // 4 // lats)])
-    scatters[1].tick(4)
-
-    later = [
-        scatters[2].collect,
-        functools.partial(
-            scatters[1].spread,
-            lambda total, sub: total[:, sub * (hid // lats) : (sub + 1) * (hid // lats)],
-        ),
-        scatters[2].end,
-        scatters[1].collect,
-        scatters[1].end,
-    ]
-
-    def attend_back(number, _):
-        window, group = number // groups, number % groups
+    scatter_up.trade(across(hid, width), p.rings)
+    mark("spread_down")
+    scatter_down.traded((ring_place(0),), ring_place(0))
+    scatter_down.spread()
+
+    def trade_up(number, _):
+        where = across(pl.multiple_of(number * chunk, 128), chunk)
+        scatter_up.traded(where, number)
+        return 0
+
+    lax.fori_loop(0, p.rings, trade_up, 0)
+    scatter_up.traded(across(hid, width), p.rings)
+    scatter_up.tick(0)
+
+    def attend_back(group, turns, number, _):
+        window = number
         at = pl.ds(pl.multiple_of(window * TOK, 16), TOK)
         query = packed[at, head_lanes(group * GROUP)]
         keyed = packed[at, head_lanes(width + group * GROUP)]
@@ -601,7 +694,9 @@
         grad_value = jnp.zeros((TOK, GROUP), F32)
         parts = []
         for h in range(per):
-            probs = probs_ref[number * per + h]
+            if h == per // 2:
+                at_turn(number, turns, 0)
+            probs = probs_ref[(number * groups + group) * per + h]
             mine = lanes == h
             grad_probs = nt(jnp.where(mine, valued, jnp.zeros_like(valued)), upstream)
             grad_value = jnp.where(mine, nn(probs.astype(BF16), upstream), grad_value)
@@ -613,17 +708,43 @@
         grad_packed[at, head_lanes(group * GROUP)] = grad_query.astype(BF16)
         grad_packed[at, head_lanes(width + group * GROUP)] = grad_key.astype(BF16)
         grad_packed[at, head_lanes(2 * width + group * GROUP)] = grad_value.astype(BF16)
-        for turn, action in enumerate(later):
-            pl.when(number == turn)(action)
+        at_turn(number, turns, 1)
         return 0
 
-    lax.fori_loop(0, 4 * groups, attend_back, 0)
-
-    def pack_back(first, number):
-        grad = tn(hidden_one[...], grad_packed[:, pl.ds(first, GROUP)])
-        scatters[0].put_at(pl.ds(first, GROUP), split_columns(grad))
-
-    columns(3 * groups, pack_back)
+    def pack_back(group):
+        def run(part, _):
+            first = pl.multiple_of(part * width + group * GROUP, GROUP)
+            grad = tn(hidden_one[...], grad_packed[:, pl.ds(first, GROUP)])
+            where = across(pl.multiple_of(part * GROUP, GROUP), GROUP)
+            scatter_packed[group].put(where, split_columns(grad))
+            return 0
+
+        lax.fori_loop(0, 3, run, 0)
+
+    turns_one = [[] for _ in range(8)]
+    turns_one[1].append(scatter_down.collect)
+    for step in range(1, steps):
+        turns_one[step + 1].append(functools.partial(scatter_up.tick, step))
+    turns_one[7].append(scatter_down.end)
+    turns_two = [[] for _ in range(8)]
+    turns_two[0].append(scatter_up.spread)
+    for step in range(1, steps):
+        turns_two[step + 1].append(functools.partial(scatter_packed[0].tick, step))
+    turns_two[3].append(scatter_up.collect)
+    turns_two[7].append(scatter_up.end)
+
+    mark("attend_back")
+    lax.fori_loop(0, 4, functools.partial(attend_back, 0, turns_one), 0)
+    mark("pack_back")
+    pack_back(0)
+    full = (every, every, every, every)
+    scatter_packed[0].trade(full, 0)
+    scatter_packed[0].traded(full, 0)
+    scatter_packed[0].tick(0)
+    mark("attend_back_two")
+    lax.fori_loop(0, 4, functools.partial(attend_back, 1, turns_two), 0)
+    mark("pack_back_two")
+    scatter_packed[0].spread()
 
     def unpack(first, number):
         share = p.rings // groups
@@ -640,30 +761,45 @@
         sums[0:8] += jnp.broadcast_to(total, (8, width))
         up_ref[at] = up_ref[at] + through
 
+    mark("norm_one_back")
     by_rows(first_back)
+    pack_back(1)
     line = lax.broadcasted_iota(jnp.int32, (128, width), 0)
     both = jnp.where(line < 64, sums[0:1], sums[8:9])
-    scatters[0].put_at(pl.ds(4 * width, 128), split_columns(jnp.transpose(both, (1, 0))))
-    scatters[0].trade(0)
+    last = scatter_packed[1]
+    last.put(across(3 * GROUP, 128), split_columns(jnp.transpose(both, (1, 0))))
+    mark("trade_last")
+    last.trade(full, 0)
+    scatter_packed[0].collect()
     send_back(up_ref, 1)
-    scatters[0].traded(0)
-    for step in range(1, scatters[0].right + 1):
-        scatters[0].tick(step)
-    share = 4 * width // lats
-    scatters[0].spread(
-        lambda total, sub: jnp.concatenate(
-            [total[:, sub * share : (sub + 1) * share], total[:, 4 * width :]], axis=1
-        )
-    )
-    scatters[0].collect()
-    scatters[0].end()
-    for sub in range(lats):
-        out_three[sub * (chunk // 4 // lats) : (sub + 1) * (chunk // 4 // lats)] = scatters[2].full[
-            sub
-        ]
-        out_two[:, sub * (hid // lats) : (sub + 1) * (hid // lats)] = scatters[1].full[sub]
-        out_one[:, sub * share : (sub + 1) * share] = scatters[0].full[sub, :, 0:share]
-    out_one[:, 4 * width :] = scatters[0].full[0, :, share:]
+    last.traded(full, 0)
+    mark("ring_last")
+    for step in range(steps):
+        last.tick(step)
+    mark("plane_last")
+    last.spread()
+
+    scatter_packed[0].end()
+
+    def store_down(at, value):
+        out_three[at] = value
+
+    def store_up(at, value):
+        out_two[at] = value
+
+    def store_packed(group, at, value):
+        for part in range(3):
+            out_one[at, part * width + group * GROUP : part * width + (group + 1) * GROUP] = value[
+                :, part * GROUP : (part + 1) * GROUP
+            ]
+        if group == 1:
+            out_one[at, 3 * width :] = value[:, 3 * GROUP :]
+
+    scatter_down.write(store_down)
+    scatter_up.write(store_up)
+    scatter_packed[0].write(functools.partial(store_packed, 0))
+    mark("collect_last")
+    last.collect()
     number = 0
     for i, j, window, quarter, down, over in shifted_blocks():
         if down or over:
@@ -674,17 +810,11 @@
                     beyond(down, over, -1),
                 )
             number += 1
+    last.end()
+    last.write(functools.partial(store_packed, 1))
+    mark("finish")
     wires.finish(p.sibling)
-
-
-def put_at(self, columns, value):
-    first, second = value[..., 0, :, :], value[..., 1, :, :]
-    mine = self.p.core == 0
-    self.own[:, :, :, columns] = jnp.where(mine, first, second)
-    self.away[:, :, :, columns] = jnp.where(mine, second, first).astype(BF16)
-
-
-Scatter.put_at = put_at
+    mark()
 
 
 def blocks_of(field):
@@ -732,18 +862,17 @@
         ],
         axis=1,
     )
-    wide = 4 * width + 128
-
-    def scatter_scratch(lines, across, piece):
+
+    def scatter_scratch(lines, across):
         return [
             pltpu.VMEM((rings, 2, lines, across), F32),
             pltpu.VMEM((rings, 2, lines, across), BF16),
             pltpu.VMEM((rings, 2, lines, across), BF16),
-            pltpu.VMEM((rings - 1, 2, lines, across), BF16),
-            pltpu.VMEM((rings - 1, 2, lines, across), BF16),
-            pltpu.VMEM((2, lats) + piece, F32),
-            pltpu.VMEM((2 * lats - 1,) + piece, F32),
-            pltpu.VMEM((lats,) + piece, F32),
+            pltpu.VMEM((2 * rings - 2, lines, across), BF16),
+            pltpu.VMEM((2 * rings - 2, lines, across), BF16),
+            pltpu.VMEM((2, lats, lines // lats, across), F32),
+            pltpu.VMEM((2 * lats - 1, lines // lats, across), F32),
+            pltpu.VMEM((lats, lines // lats, across), F32),
         ]
 
     scratch = [
@@ -766,23 +895,24 @@
         pltpu.VMEM((tokens, 3 * width), BF16),
         pltpu.VMEM((16, width), F32),
         pltpu.VMEM((16, width), F32),
-        pltpu.VMEM((rings, 2, 2, rows, wide), BF16),
+        pltpu.VMEM((rings, 2, 2, rows, 4 * width + 128), BF16),
         pltpu.VMEM((rings, 2, 2, rows, hid), BF16),
         pltpu.VMEM((rings, 2, 2, deep, width), BF16),
     ]
-    scratch += scatter_scratch(rows, wide, (rows, 4 * width // lats + 128))
-    scratch += scatter_scratch(rows, hid, (rows, hid // lats))
-    scratch += scatter_scratch(deep, width, (deep // lats, width))
-    wires = 7 + 14 + 3 * (2 * rings)
-    wires += (1 + rings - 1 + 3 * lats - 2) + 2 * (rings + rings - 1 + 3 * lats - 2)
+    scratch += scatter_scratch(deep, width)
+    scratch += scatter_scratch(rows, hid + width)
+    scratch += scatter_scratch(rows, 3 * GROUP)
+    scratch += scatter_scratch(rows, 3 * GROUP + 128)
+    wires = 14 + 14 + 3 * (3 * rings - 1)
+    wires += 4 * (2 * rings - 2 + 3 * lats - 2) + 2 * rings + 3
     scratch += [pltpu.SemaphoreType.DMA((wires,)), pltpu.SemaphoreType.DMA((wires,))]
     vmem = pl.BlockSpec(memory_space=pltpu.VMEM)
     out_field, one, two, three = pl.pallas_call(
         functools.partial(kernel, lats, lons),
         out_shape=(
             jax.ShapeDtypeStruct((4, 4, 2, PADQ, width), BF16),
-            jax.ShapeDtypeStruct((rows, wide), F32),
-            jax.ShapeDtypeStruct((rows, hid), F32),
+            jax.ShapeDtypeStruct((rows, 3 * width + 128), F32),
+            jax.ShapeDtypeStruct((rows, hid + width), F32),
             jax.ShapeDtypeStruct((deep, width), F32),
         ),
         in_specs=[vmem] * 4,
@@ -797,11 +927,11 @@
         field_of(out_field[:, :, 0]),
         field_of(out_field[:, :, 1]),
         one[:, : 3 * width],
-        one[:, 3 * width : 4 * width],
-        two,
+        two[:, hid:],
+        two[:, :hid],
         three,
-        one[:, 4 * width],
-        one[:, 4 * width + 64],
+        one[:, 3 * width],
+        one[:, 3 * width + 64],
     )
 
 

time: 206 us -> 183 us (0.89)
  Pallas kernels: 187 us -> 165 us
    pallas_call x1, Pallas kernels: 187 us -> 165 us  [body(): pl.pallas_call(functools.partial(kernel, lats, lons), out_shape=(jax.Shap...]
where the time goes in v2:
time: 183 us
  Pallas kernels  165 us (90%)
  local copies, waits for them, and re-layouts  13.3 us (7%)
  other arithmetic  3.3 us (2%)
    pallas_call x1, Pallas kernels, body(): pl.pallas_call(functools.partial(kernel, lats, lons), out_shape=(jax.Shap...  165 us

profile of v2, /device:TPU:32, one launch (start us, length us, event | category | flops | bytes accessed | tf_op | source)
XLA Modules:
  0.0 182.8 jit_solution(17197641660897160121)
XLA Ops:
  0.6 0.7 broadcast_in_dim.4
  1.4 0.7 broadcast_in_dim.5
  2.1 0.7 convert_element_type.14
  2.8 1.5 concatenate.3.shard_one
  4.3 1.3 add_convert_fusion
  5.6 0.2 reshape.45
  5.8 0.0 copy-start
  5.8 0.3 copy.22
  6.1 0.1 copy.23
  6.2 0.6 copy-done
  6.9 0.2 reshape.47
  7.1 0.3 copy.24
  7.4 0.1 copy.25
  7.5 0.2 pad_bitcast_fusion
  7.7 1.3 pad_maximum_fusion.field
  9.0 165.4 %block.1 = (bf16[4,4,2,48,512]{4,3,2,1,0:T(8,128)(2,1)}, f32[16,1664]{1,0:T(8,128)}, f32[16,2560]{1,0:T(8,128)}, f32[64,512]{1,0:T(8,128)}) custom-call(bf16[4,4,2,48,512]{4,3,2,1,0:T(8,128)(2,1)} %pad_maximum_fusion.field, bf16[16,2176]{1,0:T(8,128)(2,1)} %concatenate.3.shard_one, bf16[16,2048]{1,0:T(8,128)(2,1)} %shard_two.1, bf16[64,512]{1,0:T(8,128)(2,1)} %shard_three.1), custom_call_target="tpu_custom_call" | custom-call | tf_op jit(solution)/shard_map/block/pallas_call | solution.py:910
  174.4 1.5 slice_bitcast_fusion
  175.9 0.0 copy-start.3
  175.9 0.0 copy-start.1
  176.0 0.3 copy.28
  176.3 0.5 copy-done.3
  176.8 0.7 slice_reduce_fusion
  177.5 0.6 slice.31
  178.2 0.0 copy-done.1
  178.2 0.6 slice.32
  178.8 0.7 slice.33
  179.4 0.2 copy.29
  179.6 1.0 reshape.52
  180.7 0.3 copy.26
  181.0 0.0 copy-start.2
  181.0 0.2 copy.27
  181.2 1.0 reshape.50
  182.2 0.0 copy-done.2
  182.2 0.7 copy.31
  (2 shorter events, 0.1 us)
Async XLA Ops:
  5.8 1.1 copy-start
  175.9 0.9 copy-start.3
  175.9 2.2 %copy-start.1 = (f32[16,2560]{1,0:T(8,128)S(1)}, f32[16,2560]{1,0:T(8,128)}, u32[]{:S(2)}) copy-start(f32[16,2560]{1,0:T(8,128)} %get-tuple-element.14) | copy-start | bytes 491524
  181.0 1.2 copy-start.2

commit v3 on v2

--- a/solution.py
+++ b/solution.py
@@ -84,13 +84,9 @@
         lon = (self.lon + by_lon + self.lons) % self.lons
         return (lat, lon)
 
-    def in_plane(self, by):
-        index = (self.yh * self.lats + self.lat + by) % (2 * self.lats)
-        return index // self.lats, index % self.lats
-
-    def plane_device(self, by):
-        yh, lat = self.in_plane(by)
-        return (lat, self.z * 4 + yh * 2 + self.core)
+    def along_y(self, by):
+        y = (self.yh * 2 + self.lat % 2 + by) % 4
+        return (self.lat // 2 * 2 + y % 2, self.z * 4 + (y // 2) * 2 + self.core)
 
 
 class Wires:
@@ -194,16 +190,19 @@
 
 
 class Scatter:
-    def __init__(self, place, wires, refs, pieces):
-        self.p, self.w, self.pieces = place, wires, pieces
-        self.own, self.away, self.near, self.out, self.into, self.stage, self.land, self.full = refs
-        self.half = place.rings // 2
-        self.last = 2 * self.half - 1
+    def __init__(self, place, wires, refs, pieces, axis):
+        self.p, self.w, self.pieces, self.axis = place, wires, pieces, axis
+        self.own, self.away, self.near, self.give, self.got, self.sum = refs[:6]
+        self.out, self.into, self.stage, self.land, self.full = refs[6:]
+        self.size = {"x": place.lats // 2, "y": 4}
+        self.other = "y" if axis == "x" else "x"
+        self.count = self.sum.shape[3]
         self.exchange = wires.take(pieces)
-        self.ring = wires.take(2 * self.last)
-        self.plane = wires.take(2 * place.lats - 1)
-        self.along = wires.take(place.lats - 1)
-        self.lines = self.own.shape[2] // place.lats
+        self.over = wires.take(3)
+        self.ring = wires.take(place.rings - 1)
+        self.plane = wires.take(3)
+        self.along = wires.take(3)
+        self.x, self.y = place.lat // 2, place.yh * 2 + place.lat % 2
 
     def put(self, where, value):
         first, second = value[..., 0, :, :], value[..., 1, :, :]
@@ -223,90 +222,101 @@
         copy.wait_send()
         copy.wait_recv()
 
-    def share(self, rel, yh):
+    def at(self, axis, by):
         p = self.p
-        z = (p.z + rel + p.rings) % p.rings
-        return self.own[z, yh] + self.near[z, yh].astype(F32)
-
-    def pass_on(self, way, rel, yh):
+        size = self.size[axis]
+        if axis == "x":
+            x = (self.x + by + size) % size
+            return x, (x * 2 + p.lat % 2, p.lon)
+        y = (self.y + by + size) % size
+        return y, (self.x * 2 + y % 2, p.z * 4 + (y // 2) * 2 + p.core)
+
+    def quarter(self, number):
+        every = slice(None)
+        first = pl.multiple_of(number * self.count, 128)
+        at = (every, every, every, pl.ds(first, self.count))
+        return self.own[at] + self.near[at].astype(F32)
+
+    def cross(self):
+        for by in range(1, self.size[self.axis]):
+            number, device = self.at(self.axis, by)
+            self.give[by - 1] = self.quarter(number).astype(BF16)
+            source = self.give.at[by - 1]
+            self.w.start(
+                source, self.got.at[by - 1], self.over + by - 1, device, lambda: self.give.at[0]
+            )
+
+    def crossed(self):
         p = self.p
-        base = 0 if way > 0 else self.last
-        slot = base + 2 * rel - 2 + yh if rel < self.half else base + self.last - 1
-        total = self.share(way * rel, yh)
-        longest = self.half if (yh == 0) == (way > 0) else self.half - 1
-        if rel < longest:
-            before = base + 2 * rel + yh if rel + 1 < self.half else base + self.last - 1
-            self.w.landed(self.into.at[before], self.ring + before, p.along_z(-way))
-            total = total + self.into[before].astype(F32)
-        self.out[slot] = total.astype(BF16)
-        self.w.start(
-            self.out.at[slot],
-            self.into.at[slot],
-            self.ring + slot,
-            p.along_z(way),
-            lambda: self.out.at[0],
-        )
-
-    def tick(self, step):
-        if step == 0:
-            self.pass_on(1, self.half, 0)
-            self.pass_on(-1, self.half, 1)
-            self.pass_on(1, self.half - 1, 1)
-            self.pass_on(-1, self.half - 1, 0)
-        else:
-            rel = self.half - (step + 1) // 2
-            first = step % 2
-            if not first:
-                rel -= 1
-            if rel < 1:
-                return
-            self.pass_on(1, rel, 0 if first else 1)
-            self.pass_on(-1, rel, 1 if first else 0)
+        total = self.quarter(self.at(self.axis, 0)[0])
+        for by in range(1, self.size[self.axis]):
+            device = self.at(self.axis, -by)[1]
+            self.w.landed(self.got.at[by - 1], self.over + by - 1, device)
+            total = total + self.got[by - 1].astype(F32)
+        self.sum[...] = total
+        for by in range(1, p.rings):
+            self.out[by - 1] = self.sum[(p.z + by) % p.rings].astype(BF16)
+            source = self.out.at[by - 1]
+            self.w.start(
+                source,
+                self.into.at[by - 1],
+                self.ring + by - 1,
+                p.along_z(by),
+                lambda: self.out.at[0],
+            )
 
     def spread(self):
         p = self.p
-        for yh in range(2):
-            total = self.share(0, yh)
-            for way in (1, -1):
-                slot = yh if way > 0 else self.last + yh
-                self.w.landed(self.into.at[slot], self.ring + slot, p.along_z(-way))
-                total = total + self.into[slot].astype(F32)
-            for sub in range(p.lats):
-                self.stage[yh, sub] = total[sub * self.lines : (sub + 1) * self.lines]
-        for by in range(1, 2 * p.lats):
-            yh, lat = p.in_plane(by)
+        total = self.sum[p.z]
+        for by in range(1, p.rings):
+            self.w.landed(self.into.at[by - 1], self.ring + by - 1, p.along_z(-by))
+            total = total + self.into[by - 1].astype(F32)
+        self.stage[...] = total
+        here = self.at(self.other, 0)[0]
+        self.land[here] = self.stage[...]
+        for by in range(1, self.size[self.other]):
+            device = self.at(self.other, by)[1]
             self.w.start(
-                self.stage.at[yh, lat],
-                self.land.at[by - 1],
+                self.stage,
+                self.land.at[here],
                 self.plane + by - 1,
-                p.plane_device(by),
+                device,
                 lambda: self.land.at[0],
             )
 
     def collect(self):
         p = self.p
-        total = self.stage[p.yh, p.lat]
-        for by in range(1, 2 * p.lats):
-            self.w.landed(
-                self.land.at[by - 1], self.plane + by - 1, p.plane_device(2 * p.lats - by)
+        size = self.size[self.other]
+        for by in range(1, size):
+            number, device = self.at(self.other, -by)
+            self.w.landed(self.land.at[number], self.plane + by - 1, device)
+        total = self.land[0]
+        for number in range(1, size):
+            total = total + self.land[number]
+        mine = self.at(self.other, 0)[0]
+        self.land[mine] = total
+        here = self.at(self.axis, 0)[0]
+        self.full[here] = self.land[mine, p.yh]
+        for by in range(1, self.size[self.axis]):
+            number, device = self.at(self.axis, by)
+            yh = p.yh if self.axis == "x" else number // 2
+            self.w.start(
+                self.land.at[mine, yh],
+                self.full.at[here],
+                self.along + by - 1,
+                device,
+                lambda: self.full.at[0],
             )
-            total = total + self.land[by - 1]
-        self.full[p.lat] = total
-        block = self.full.at[p.lat]
-        for by in range(1, p.lats):
-            self.w.start(
-                block, block, self.along + by - 1, p.moved(by, 0), lambda: self.full.at[0]
-            )
 
     def end(self):
-        p = self.p
-        for by in range(1, p.lats):
-            lat = (p.lat - by + p.lats) % p.lats
-            self.w.landed(self.full.at[lat], self.along + by - 1, (lat, p.lon))
-
-    def write(self, store):
-        for sub in range(self.p.lats):
-            store(slice(sub * self.lines, (sub + 1) * self.lines), self.full[sub])
+        for by in range(1, self.size[self.axis]):
+            number, device = self.at(self.axis, -by)
+            self.w.landed(self.full.at[number], self.along + by - 1, device)
+
+    def columns(self):
+        return jnp.concatenate(
+            [self.full[number] for number in range(self.size[self.axis])], axis=1
+        )
 
 
 def shifted_blocks():
@@ -368,9 +378,11 @@
     mark = Marks()
     mark("barrier")
     barrier = pltpu.get_barrier_semaphore()
-    friends = [p.plane_device(by) for by in range(1, 2 * lats)]
-    friends += [p.sibling, p.along_z(1), p.along_z(-1)]
-    friends += [p.moved(0, 1), p.moved(0, -1), p.moved(1, 1), p.moved(-1, -1)]
+    friends = [p.sibling] + [p.along_z(by) for by in range(1, p.rings)]
+    friends += [p.moved(2 * by, 0) for by in range(1, lats // 2)]
+    friends += [p.along_y(by) for by in range(1, 4)]
+    for by_lat, by_lon in ((1, 0), (0, 1), (1, 1)):
+        friends += [p.moved(by_lat, by_lon), p.moved(-by_lat, -by_lon)]
     for friend in friends:
         pl.semaphore_signal(barrier, inc=1, device_id=friend, device_id_type=MESH)
     pl.semaphore_wait(barrier, len(friends))
@@ -414,21 +426,17 @@
 
     first_weight.tick(0)
     send_halo(0)
-    first_weight.tick(1)
-    assemble(0, (0,), x_ref)
-    first_weight.tick(2)
-    first_weight.tick(3)
-    assemble(0, (1, 2), x_ref)
-    first_weight.tick(4)
-    first_weight.tick(5)
-    assemble(0, (3,), x_ref)
-    for step in range(6, first_weight.last + 1):
+    for step in range(1, first_weight.last):
         first_weight.tick(step)
     second_weight.tick(0)
+    third_weight.tick(0)
+    first_weight.tick(first_weight.last)
+    second_weight.tick(1)
+    third_weight.tick(1)
     send_halo(1)
-    second_weight.tick(1)
     mark("gather_one_end")
     first_weight.end()
+    assemble(0, (0, 1, 2, 3), x_ref)
 
     def weight(ref, first, count):
         return ref[:, :, :, :, pl.ds(first, count)].reshape(width, count)
@@ -486,11 +494,16 @@
                 pl.when(number == turn // 2)(act)
 
     turns = [[] for _ in range(8 * groups)]
-    for step in range(2, second_weight.last + 1):
-        turns[2 * step - 3].append(functools.partial(second_weight.tick, step))
-    turns[11].append(functools.partial(third_weight.tick, 0))
-    turns[13].append(functools.partial(third_weight.tick, 1))
-    turns[15].append(functools.partial(third_weight.tick, 2))
+    for step in range(2, min(6, second_weight.last)):
+        turns[4 * step - 7] += [
+            functools.partial(second_weight.tick, step),
+            functools.partial(third_weight.tick, step),
+        ]
+
+    def weights_tick(step):
+        if step <= second_weight.last:
+            second_weight.tick(step)
+            third_weight.tick(step)
 
     def attend(number, _):
         window, group = number // groups, number % groups
@@ -519,7 +532,6 @@
 
     lax.fori_loop(0, 4 * groups, attend, 0)
     mark("project")
-    third_weight.tick(3)
 
     def project(first, number):
         middle[:, pl.ds(first, GROUP)] = x_ref[0:tokens, pl.ds(first, GROUP)] + nn(
@@ -527,9 +539,8 @@
         )
 
     columns(groups, project)
-    third_weight.tick(4)
+    weights_tick(6)
     assemble(1, (0, 1, 2, 3), up_ref)
-    third_weight.tick(5)
 
     def second_norm(at):
         normed, _ = layer_norm(middle[at])
@@ -538,16 +549,20 @@
 
     by_rows(second_norm)
     mark("gather_end")
-    for step in range(6, third_weight.last + 1):
-        third_weight.tick(step)
+    if second_weight.last < 6:
+        weights_tick(second_weight.last)
+    weights_tick(7)
+    weights_tick(8)
     second_weight.end()
     third_weight.end()
 
-    scatter_down = Scatter(p, wires, scatter_refs[0:8], p.rings)
-    scatter_up = Scatter(p, wires, scatter_refs[8:16], p.rings + 1)
-    scatter_packed = [
-        Scatter(p, wires, scatter_refs[16 + 8 * k : 24 + 8 * k], 1) for k in range(groups)
-    ]
+    def scatter(number, pieces, axis):
+        return Scatter(p, wires, scatter_refs[11 * number : 11 * number + 11], pieces, axis)
+
+    scatter_down = scatter(0, p.rings, "y")
+    scatter_up = scatter(1, p.rings + 1, "x")
+    scatter_query = [scatter(2, 1, "y"), scatter(3, 1, "x")]
+    scatter_value = [scatter(4, 1, "x"), scatter(5, 1, "y")]
     every = slice(None)
 
     def across(first, count):
@@ -555,18 +570,6 @@
 
     def ring_place(rel):
         return (p.z + rel + p.rings) % p.rings
-
-    def down_tick(step):
-        if step % 2 == 0:
-            needed = (p.rings // 2,) if step == 0 else ()
-            near = p.rings // 2 - 1 - step // 2
-            for rel in needed + (near, -near):
-                place = ring_place(rel)
-                scatter_down.traded((place,), place)
-        scatter_down.tick(step)
-
-    steps = p.rings - 2
-    turns_feed = ((max(2, p.rings // 2 - 1), 0), (p.rings - 2, 1), (p.rings - 1, 2))
 
     def feed(number, _):
         rel = jnp.where(
@@ -590,9 +593,6 @@
         where = across(pl.multiple_of(place * chunk, 128), chunk)
         scatter_up.put(where, grad_up.reshape(p.rings, 2, 2, rows, chunk))
         scatter_up.trade(where, place)
-        for turn, step in turns_feed:
-            if step < steps:
-                pl.when(number == turn)(functools.partial(down_tick, step))
         return 0
 
     mark("feed")
@@ -604,10 +604,13 @@
             active[...], down
         )
 
+    def trade_all(number, _):
+        scatter_down.traded((number,), number)
+        scatter_up.traded(across(pl.multiple_of(number * chunk, 128), chunk), number)
+        return 0
+
     mark("lower")
     columns(groups, lower)
-    for step in range(3, min(steps, 4)):
-        down_tick(step)
 
     returns = wires.take(14)
 
@@ -628,8 +631,8 @@
 
     mark("return_out")
     send_back(result, 0)
-    for step in range(4, min(steps, 5)):
-        down_tick(step)
+    lax.fori_loop(0, p.rings, trade_all, 0)
+    scatter_down.cross()
 
     def raise_back(first, number):
         share = p.rings // groups
@@ -638,8 +641,6 @@
 
     mark("raise_back")
     columns(groups, raise_back)
-    for step in range(5, steps):
-        down_tick(step)
 
     sums[...] = jnp.zeros_like(sums)
 
@@ -669,18 +670,6 @@
     mark("project_back")
     columns(groups, project_back)
     scatter_up.trade(across(hid, width), p.rings)
-    mark("spread_down")
-    scatter_down.traded((ring_place(0),), ring_place(0))
-    scatter_down.spread()
-
-    def trade_up(number, _):
-        where = across(pl.multiple_of(number * chunk, 128), chunk)
-        scatter_up.traded(where, number)
-        return 0
-
-    lax.fori_loop(0, p.rings, trade_up, 0)
-    scatter_up.traded(across(hid, width), p.rings)
-    scatter_up.tick(0)
 
     def attend_back(group, turns, number, _):
         window = number
@@ -716,35 +705,44 @@
             first = pl.multiple_of(part * width + group * GROUP, GROUP)
             grad = tn(hidden_one[...], grad_packed[:, pl.ds(first, GROUP)])
             where = across(pl.multiple_of(part * GROUP, GROUP), GROUP)
-            scatter_packed[group].put(where, split_columns(grad))
+            scatter_query[group].put(where, split_columns(grad))
             return 0
 
-        lax.fori_loop(0, 3, run, 0)
+        lax.fori_loop(0, 2, run, 0)
+        scatter_query[group].trade(full, 0)
+        first = 2 * width + group * GROUP
+        grad = tn(hidden_one[...], grad_packed[:, first : first + GROUP])
+        scatter_value[group].put(across(0, GROUP), split_columns(grad))
+
+    full = (every, every, every, every)
+
+    def up_cross():
+        scatter_up.traded(across(hid, width), p.rings)
+        scatter_up.cross()
+
+    def packed_cross(group):
+        scatter_query[group].traded(full, 0)
+        scatter_query[group].cross()
+        scatter_value[group].traded(full, 0)
+        scatter_value[group].cross()
 
     turns_one = [[] for _ in range(8)]
-    turns_one[1].append(scatter_down.collect)
-    for step in range(1, steps):
-        turns_one[step + 1].append(functools.partial(scatter_up.tick, step))
-    turns_one[7].append(scatter_down.end)
+    turns_one[2].append(up_cross)
     turns_two = [[] for _ in range(8)]
-    turns_two[0].append(scatter_up.spread)
-    for step in range(1, steps):
-        turns_two[step + 1].append(functools.partial(scatter_packed[0].tick, step))
-    turns_two[3].append(scatter_up.collect)
-    turns_two[7].append(scatter_up.end)
+    turns_two[1].append(scatter_down.crossed)
+    turns_two[3].append(functools.partial(packed_cross, 0))
 
     mark("attend_back")
     lax.fori_loop(0, 4, functools.partial(attend_back, 0, turns_one), 0)
     mark("pack_back")
     pack_back(0)
-    full = (every, every, every, every)
-    scatter_packed[0].trade(full, 0)
-    scatter_packed[0].traded(full, 0)
-    scatter_packed[0].tick(0)
+    scatter_value[0].put(across(GROUP, GROUP), jnp.zeros((p.rings, 2, 2, rows, GROUP), F32))
+    scatter_value[0].trade(full, 0)
     mark("attend_back_two")
     lax.fori_loop(0, 4, functools.partial(attend_back, 1, turns_two), 0)
     mark("pack_back_two")
-    scatter_packed[0].spread()
+    pack_back(1)
+    scatter_up.crossed()
 
     def unpack(first, number):
         share = p.rings // groups
@@ -754,6 +752,7 @@
         )
 
     columns(groups, unpack)
+    scatter_down.spread()
 
     def first_back(at):
         normed, inverse = layer_norm(x_ref[at])
@@ -763,43 +762,55 @@
 
     mark("norm_one_back")
     by_rows(first_back)
-    pack_back(1)
     line = lax.broadcasted_iota(jnp.int32, (128, width), 0)
     both = jnp.where(line < 64, sums[0:1], sums[8:9])
-    last = scatter_packed[1]
-    last.put(across(3 * GROUP, 128), split_columns(jnp.transpose(both, (1, 0))))
+    gain_sums = jnp.transpose(both, (1, 0))
+    gain_sums = jnp.concatenate([gain_sums, gain_sums], axis=1)
+    scatter_value[1].put(across(GROUP, GROUP), split_columns(gain_sums))
     mark("trade_last")
-    last.trade(full, 0)
-    scatter_packed[0].collect()
+    scatter_value[1].trade(full, 0)
+    scatter_query[1].traded(full, 0)
+    scatter_query[1].cross()
     send_back(up_ref, 1)
-    last.traded(full, 0)
-    mark("ring_last")
-    for step in range(steps):
-        last.tick(step)
-    mark("plane_last")
-    last.spread()
-
-    scatter_packed[0].end()
-
-    def store_down(at, value):
-        out_three[at] = value
-
-    def store_up(at, value):
-        out_two[at] = value
-
-    def store_packed(group, at, value):
-        for part in range(3):
-            out_one[at, part * width + group * GROUP : part * width + (group + 1) * GROUP] = value[
-                :, part * GROUP : (part + 1) * GROUP
-            ]
+    scatter_value[1].traded(full, 0)
+    scatter_value[1].cross()
+    mark("last")
+    for early in (scatter_query[0], scatter_value[0]):
+        early.crossed()
+    scatter_down.collect()
+    scatter_up.spread()
+    scatter_query[0].spread()
+    scatter_value[0].spread()
+    scatter_query[1].crossed()
+    scatter_value[1].crossed()
+    scatter_down.end()
+    scatter_up.collect()
+    scatter_query[0].collect()
+    scatter_value[0].collect()
+    scatter_query[1].spread()
+    scatter_value[1].spread()
+    scatter_up.end()
+    scatter_query[0].end()
+    scatter_value[0].end()
+
+    def write_packed(group):
+        here = group * GROUP
+        value = scatter_query[group].columns()
+        out_one[:, here : here + GROUP] = value[:, :GROUP]
+        out_one[:, width + here : width + here + GROUP] = value[:, GROUP:]
+        value = scatter_value[group].columns()
+        out_one[:, 2 * width + here : 2 * width + here + GROUP] = value[:, :GROUP]
         if group == 1:
-            out_one[at, 3 * width :] = value[:, 3 * GROUP :]
-
-    scatter_down.write(store_down)
-    scatter_up.write(store_up)
-    scatter_packed[0].write(functools.partial(store_packed, 0))
+            out_one[:, 4 * width :] = value[:, GROUP : GROUP + 128]
+
+    out_three[...] = scatter_down.columns()
+    value = scatter_up.columns()
+    out_two[...] = value[:, :hid]
+    out_one[:, 3 * width : 4 * width] = value[:, hid:]
+    write_packed(0)
     mark("collect_last")
-    last.collect()
+    scatter_query[1].collect()
+    scatter_value[1].collect()
     number = 0
     for i, j, window, quarter, down, over in shifted_blocks():
         if down or over:
@@ -810,8 +821,9 @@
                     beyond(down, over, -1),
                 )
             number += 1
-    last.end()
-    last.write(functools.partial(store_packed, 1))
+    scatter_query[1].end()
+    scatter_value[1].end()
+    write_packed(1)
     mark("finish")
     wires.finish(p.sibling)
     mark()
@@ -864,15 +876,19 @@
     )
 
     def scatter_scratch(lines, across):
+        quarter = across // 4
         return [
             pltpu.VMEM((rings, 2, lines, across), F32),
             pltpu.VMEM((rings, 2, lines, across), BF16),
             pltpu.VMEM((rings, 2, lines, across), BF16),
-            pltpu.VMEM((2 * rings - 2, lines, across), BF16),
-            pltpu.VMEM((2 * rings - 2, lines, across), BF16),
-            pltpu.VMEM((2, lats, lines // lats, across), F32),
-            pltpu.VMEM((2 * lats - 1, lines // lats, across), F32),
-            pltpu.VMEM((lats, lines // lats, across), F32),
+            pltpu.VMEM((3, rings, 2, lines, quarter), BF16),
+            pltpu.VMEM((3, rings, 2, lines, quarter), BF16),
+            pltpu.VMEM((rings, 2, lines, quarter), F32),
+            pltpu.VMEM((rings - 1, 2, lines, quarter), BF16),
+            pltpu.VMEM((rings - 1, 2, lines, quarter), BF16),
+            pltpu.VMEM((2, lines, quarter), F32),
+            pltpu.VMEM((4, 2, lines, quarter), F32),
+            pltpu.VMEM((4, lines, quarter), F32),
         ]
 
     scratch = [
@@ -901,18 +917,17 @@
     ]
     scratch += scatter_scratch(deep, width)
     scratch += scatter_scratch(rows, hid + width)
-    scratch += scatter_scratch(rows, 3 * GROUP)
-    scratch += scatter_scratch(rows, 3 * GROUP + 128)
-    wires = 14 + 14 + 3 * (3 * rings - 1)
-    wires += 4 * (2 * rings - 2 + 3 * lats - 2) + 2 * rings + 3
+    for _ in range(4):
+        scratch += scatter_scratch(rows, 2 * GROUP)
+    wires = 14 + 14 + 3 * (3 * rings - 1) + 6 * (rings - 1 + 9) + 2 * rings + 5
     scratch += [pltpu.SemaphoreType.DMA((wires,)), pltpu.SemaphoreType.DMA((wires,))]
     vmem = pl.BlockSpec(memory_space=pltpu.VMEM)
     out_field, one, two, three = pl.pallas_call(
         functools.partial(kernel, lats, lons),
         out_shape=(
             jax.ShapeDtypeStruct((4, 4, 2, PADQ, width), BF16),
-            jax.ShapeDtypeStruct((rows, 3 * width + 128), F32),
-            jax.ShapeDtypeStruct((rows, hid + width), F32),
+            jax.ShapeDtypeStruct((rows, 4 * width + 128), F32),
+            jax.ShapeDtypeStruct((rows, hid), F32),
             jax.ShapeDtypeStruct((deep, width), F32),
         ),
         in_specs=[vmem] * 4,
@@ -927,11 +942,11 @@
         field_of(out_field[:, :, 0]),
         field_of(out_field[:, :, 1]),
         one[:, : 3 * width],
-        two[:, hid:],
-        two[:, :hid],
+        one[:, 3 * width : 4 * width],
+        two,
         three,
-        one[:, 3 * width],
-        one[:, 3 * width + 64],
+        one[:, 4 * width],
+        one[:, 4 * width + 64],
     )
 
 

time: 183 us -> 150 us (0.82)
  Pallas kernels: 165 us -> 132 us
    pallas_call x1, Pallas kernels: 165 us -> 132 us  [body(): pl.pallas_call(functools.partial(kernel, lats, lons), out_shape=(jax.Shap...]
where the time goes in v3:
time: 150 us; the launch traced here: 149 us
  Pallas kernels  132 us (88%)
  local copies, waits for them, and re-layouts  13.3 us (9%)
  other arithmetic  3.3 us (2%)
    pallas_call x1, Pallas kernels, body(): pl.pallas_call(functools.partial(kernel, lats, lons), out_shape=(jax.Shap...  132 us

profile of v3, /device:TPU:32, one launch (start us, length us, event | category | flops | bytes accessed | tf_op | source)
XLA Modules:
  0.0 149.0 jit_solution(89913276573443780)
XLA Ops:
  0.6 0.7 broadcast_in_dim.4
  1.4 0.7 broadcast_in_dim.5
  2.1 0.7 convert_element_type.14
  2.8 1.5 %concatenate.3.shard_one = bf16[16,2176]{1,0:T(8,128)(2,1)} concatenate(bf16[16,1536]{1,0:T(8,128)(2,1)} %param.14, bf16[16,512]{1,0:T(8,128)(2,1)} %param.15, bf16[16,64]{1,0:T(8,128)(2,1)S(1)} %broadcast_in_dim.4, bf16[16,64]{1,0:T(8,128)(2,1)S(1)} %broadcast_in_dim.5), dimensions={1} | concatenate | bytes 139264 | tf_op jit(solution)/shard_map/concatenate | solution.py:868
  4.3 1.3 add_convert_fusion
  5.6 0.2 reshape.45
  5.8 0.0 copy-start
  5.8 0.3 copy.22
  6.1 0.1 copy.23
  6.2 0.6 copy-done
  6.9 0.2 reshape.47
  7.1 0.3 copy.24
  7.4 0.1 copy.25
  7.5 0.2 pad_bitcast_fusion
  7.7 1.3 pad_maximum_fusion.field
  9.0 131.5 %block.1 = (bf16[4,4,2,48,512]{4,3,2,1,0:T(8,128)(2,1)}, f32[16,2176]{1,0:T(8,128)}, f32[16,2048]{1,0:T(8,128)}, f32[64,512]{1,0:T(8,128)}) custom-call(bf16[4,4,2,48,512]{4,3,2,1,0:T(8,128)(2,1)} %pad_maximum_fusion.field, bf16[16,2176]{1,0:T(8,128)(2,1)} %concatenate.3.shard_one, bf16[16,2048]{1,0:T(8,128)(2,1)} %shard_two.1, bf16[64,512]{1,0:T(8,128)(2,1)} %shard_three.1), custom_call_target="tpu_custom_call" | custom-call | tf_op jit(solution)/shard_map/block/pallas_call | solution.py:925
  140.5 1.5 slice_bitcast_fusion
  142.0 0.0 copy-start.1
  142.1 0.3 copy.28
  142.4 0.5 copy-done.1
  142.9 0.7 slice_reduce_fusion
  143.6 0.6 slice.29
  144.3 0.6 slice.28
  144.9 0.2 copy.29
  145.1 1.0 reshape.52
  146.1 0.3 copy.26
  146.4 0.0 copy-start.3
  146.5 0.0 copy-start.2
  146.5 0.2 copy.27
  146.6 1.0 reshape.50
  147.6 0.0 copy-done.3
  147.6 0.7 copy.32
  148.3 0.0 copy-done.2
  148.3 0.7 copy.33
  (2 shorter events, 0.1 us)
Async XLA Ops:
  5.8 1.1 copy-start
  142.0 0.9 copy-start.1
  146.4 1.2 copy-start.3
  146.5 1.8 %copy-start.2 = (f32[64,512]{1,0:T(8,128)S(1)}, f32[64,512]{1,0:T(8,128)}, u32[]{:S(2)}) copy-start(f32[64,512]{1,0:T(8,128)} %get-tuple-element.35) | copy-start | bytes 393220

commit v4 on v3

--- a/solution.py
+++ b/solution.py
@@ -75,18 +75,38 @@
         near = self.lat + 1 - 2 * (self.lat % 2)
         self.partner = (near, self.z * 4 + (1 - self.yh) * 2 + self.core)
 
+        self.zs = [self.z] + [(self.z + by) % self.rings for by in range(1, self.rings)]
+        side = self.yh * 2 + self.core
+        self.on_z = [(self.lat, z * 4 + side) for z in self.zs]
+        steps = ((0, 1), (1, 0), (1, 1))
+        self.around = {}
+        for by_lat, by_lon in steps:
+            ahead = ((self.lat + by_lat) % lats, (self.lon + by_lon) % lons)
+            behind = ((self.lat - by_lat + lats) % lats, (self.lon - by_lon + lons) % lons)
+            self.around[by_lat, by_lon] = ahead
+            self.around[-by_lat, -by_lon] = behind
+        self.size = {"x": lats // 2, "y": 4}
+        x, low = self.lat // 2, self.lat % 2
+        xs = [x] + [(x + by) % (lats // 2) for by in range(1, lats // 2)]
+        y = self.yh * 2 + low
+        ys = [y] + [(y + by) % 4 for by in range(1, 4)]
+        here = self.z * 4 + self.core
+        self.on = {
+            "x": [(number, (number * 2 + low, self.lon)) for number in xs],
+            "y": [(number, (x * 2 + number % 2, here + number // 2 * 2)) for number in ys],
+        }
+
+    def z_of(self, by):
+        return self.zs[by % self.rings]
+
     def along_z(self, by):
-        z = (self.z + by + self.rings) % self.rings
-        return (self.lat, z * 4 + self.yh * 2 + self.core)
+        return self.on_z[by % self.rings]
 
     def moved(self, by_lat, by_lon):
-        lat = (self.lat + by_lat + self.lats) % self.lats
-        lon = (self.lon + by_lon + self.lons) % self.lons
-        return (lat, lon)
-
-    def along_y(self, by):
-        y = (self.yh * 2 + self.lat % 2 + by) % 4
-        return (self.lat // 2 * 2 + y % 2, self.z * 4 + (y // 2) * 2 + self.core)
+        return self.around[by_lat, by_lon]
+
+    def at(self, axis, by):
+        return self.on[axis][by % self.size[axis]]
 
 
 class Wires:
@@ -134,11 +154,11 @@
     def slot(self, rel, other):
         p = self.p
         yh = 1 - p.yh if other else p.yh
-        return self.whole.at[(p.z - rel + p.rings) % p.rings, yh, p.core]
+        return self.whole.at[p.z_of(-rel), yh, p.core]
 
     def pair(self, rel, core):
         p = self.p
-        return self.whole.at[(p.z - rel + p.rings) % p.rings, :, core]
+        return self.whole.at[p.z_of(-rel), :, core]
 
     def forward(self, way, hop, other):
         if hop == self.half - 1 and other != (way < 0):
@@ -189,12 +209,84 @@
             self.w.landed(self.pair(rel, 1 - p.core), self.side + rel, p.sibling)
 
 
+class Quarters(Gather):
+    def __init__(self, place, wires, shard, whole, axis):
+        super().__init__(place, wires, shard, whole)
+        self.axis = axis
+        self.size = place.size[axis]
+        self.count = shard.shape[1] // self.size
+        self.over = wires.take(self.size - 1)
+        self.mine = self.span(self.p.at(axis, 0)[0])
+        partner = place.partner[0] % 2 + 2 * (1 - place.yh) if axis == "y" else place.lat // 2
+        self.theirs = self.span(partner)
+
+    def span(self, number):
+        return pl.ds(pl.multiple_of(number * self.count, 128), self.count)
+
+    def slot(self, rel, other):
+        p = self.p
+        yh = 1 - p.yh if other else p.yh
+        return self.whole.at[p.z_of(-rel), yh, p.core, :, self.mine]
+
+    def all_of(self, core, by):
+        return self.whole.at[:, :, core, :, self.span(self.p.at(self.axis, by)[0])]
+
+    def forward(self, way, hop, other):
+        if hop == self.half - 1 and other != (way < 0):
+            return
+        index = self.way[way] + (2 * hop + other if hop < self.half - 1 else 2 * hop)
+        block = self.slot(way * hop, other)
+        self.w.start(block, block, index, self.p.along_z(way), lambda: self.slot(0, 0))
+
+    def share(self, rel):
+        pass
+
+    def begin(self):
+        p = self.p
+        self.whole[p.z, p.yh, p.core, :, self.mine] = self.shard[:, self.mine]
+        for way in (1, -1):
+            self.forward(way, 0, 0)
+        self.w.start(
+            self.shard.at[:, self.theirs],
+            self.whole.at[p.z, p.yh, p.core, :, self.theirs],
+            self.far,
+            p.partner,
+            lambda: self.shard.at[:, self.mine],
+        )
+
+    def tick(self, step):
+        if step == 0:
+            self.begin()
+        else:
+            super().tick(step)
+
+    def view(self):
+        return self.all_of(self.p.core, 0)
+
+    def exchange(self):
+        block = self.view()
+        self.w.start(block, block, self.side, self.p.sibling, self.view)
+        for by in range(1, self.size):
+            device = self.p.at(self.axis, by)[1]
+            self.w.start(block, block, self.over + by - 1, device, self.view)
+
+    def arrive(self):
+        for by in range(1, self.size):
+            block = self.all_of(self.p.core, -by)
+            self.w.landed(block, self.over + by - 1, self.p.at(self.axis, -by)[1])
+            self.w.start(block, block, self.side + by, self.p.sibling, self.view)
+
+    def end(self):
+        for by in range(self.size):
+            self.w.landed(self.all_of(1 - self.p.core, -by), self.side + by, self.p.sibling)
+
+
 class Scatter:
     def __init__(self, place, wires, refs, pieces, axis):
         self.p, self.w, self.pieces, self.axis = place, wires, pieces, axis
         self.own, self.away, self.near, self.give, self.got, self.sum = refs[:6]
         self.out, self.into, self.stage, self.land, self.full = refs[6:]
-        self.size = {"x": place.lats // 2, "y": 4}
+        self.size = place.size
         self.other = "y" if axis == "x" else "x"
         self.count = self.sum.shape[3]
         self.exchange = wires.take(pieces)
@@ -202,7 +294,6 @@
         self.ring = wires.take(place.rings - 1)
         self.plane = wires.take(3)
         self.along = wires.take(3)
-        self.x, self.y = place.lat // 2, place.yh * 2 + place.lat % 2
 
     def put(self, where, value):
         first, second = value[..., 0, :, :], value[..., 1, :, :]
@@ -223,13 +314,7 @@
         copy.wait_recv()
 
     def at(self, axis, by):
-        p = self.p
-        size = self.size[axis]
-        if axis == "x":
-            x = (self.x + by + size) % size
-            return x, (x * 2 + p.lat % 2, p.lon)
-        y = (self.y + by + size) % size
-        return y, (self.x * 2 + y % 2, p.z * 4 + (y // 2) * 2 + p.core)
+        return self.p.at(axis, by)
 
     def quarter(self, number):
         every = slice(None)
@@ -255,7 +340,7 @@
             total = total + self.got[by - 1].astype(F32)
         self.sum[...] = total
         for by in range(1, p.rings):
-            self.out[by - 1] = self.sum[(p.z + by) % p.rings].astype(BF16)
+            self.out[by - 1] = self.sum[p.z_of(by)].astype(BF16)
             source = self.out.at[by - 1]
             self.w.start(
                 source,
@@ -330,11 +415,15 @@
 def kernel(
     lats,
     lons,
-    field,
-    shard_one,
+    cells_in,
+    cotangent_in,
+    qkv_shard,
+    proj_shard,
+    gain_shard,
     shard_two,
     shard_three,
-    out_field,
+    out_block,
+    out_grad,
     out_one,
     out_two,
     out_three,
@@ -357,6 +446,7 @@
     grad_packed,
     gains,
     sums,
+    shard_one,
     one,
     two,
     three,
@@ -377,10 +467,12 @@
 
     mark = Marks()
     mark("barrier")
+    shard_one[:, : 3 * width] = qkv_shard[...]
+    shard_one[:, 3 * width : 4 * width] = proj_shard[...]
+    shard_one[:, 4 * width :] = gain_shard[...]
     barrier = pltpu.get_barrier_semaphore()
     friends = [p.sibling] + [p.along_z(by) for by in range(1, p.rings)]
-    friends += [p.moved(2 * by, 0) for by in range(1, lats // 2)]
-    friends += [p.along_y(by) for by in range(1, 4)]
+    friends += [p.at(axis, by)[1] for axis in ("x", "y") for by in range(1, p.size[axis])]
     for by_lat, by_lon in ((1, 0), (0, 1), (1, 1)):
         friends += [p.moved(by_lat, by_lon), p.moved(-by_lat, -by_lon)]
     for friend in friends:
@@ -392,16 +484,16 @@
 
     mark("gather_one")
     halo = wires.take(14)
+    fields, outs = (cells_in, cotangent_in), (out_block, out_grad)
     edge = [item for item in shifted_blocks() if item[4] or item[5]]
-    first_weight, second_weight, third_weight = [
-        Gather(p, wires, shard, whole)
-        for shard, whole in ((shard_one, one), (shard_two, two), (shard_three, three))
-    ]
+    first_weight = Gather(p, wires, shard_one, one)
+    second_weight = Quarters(p, wires, shard_two, two, "x")
+    third_weight = Quarters(p, wires, shard_three, three, "y")
 
     def send_halo(kind):
         for number, (i, j, window, quarter, down, over) in enumerate(edge):
             wires.start(
-                field.at[(i + 1) % 4, (j + 1) % 4, kind],
+                fields[kind].at[(i + 1) % 4, (j + 1) % 4],
                 moved.at[window, quarter, kind],
                 halo + 7 * kind + number,
                 beyond(down, over, -1),
@@ -421,18 +513,19 @@
                 )
                 block = moved[window, quarter, kind]
             else:
-                block = field[i + 1, j + 1, kind]
+                block = fields[kind][i + 1, j + 1]
             target[pl.ds(TOK * window + QUAD * quarter, PADQ)] = block.astype(F32)
 
     first_weight.tick(0)
     send_halo(0)
-    for step in range(1, first_weight.last):
-        first_weight.tick(step)
     second_weight.tick(0)
     third_weight.tick(0)
-    first_weight.tick(first_weight.last)
-    second_weight.tick(1)
-    third_weight.tick(1)
+    for step in range(1, first_weight.last + 1):
+        first_weight.tick(step)
+        second_weight.tick(step)
+        third_weight.tick(step)
+    second_weight.exchange()
+    third_weight.exchange()
     send_halo(1)
     mark("gather_one_end")
     first_weight.end()
@@ -494,16 +587,8 @@
                 pl.when(number == turn // 2)(act)
 
     turns = [[] for _ in range(8 * groups)]
-    for step in range(2, min(6, second_weight.last)):
-        turns[4 * step - 7] += [
-            functools.partial(second_weight.tick, step),
-            functools.partial(third_weight.tick, step),
-        ]
-
-    def weights_tick(step):
-        if step <= second_weight.last:
-            second_weight.tick(step)
-            third_weight.tick(step)
+    turns[14].append(second_weight.arrive)
+    turns[15].append(third_weight.arrive)
 
     def attend(number, _):
         window, group = number // groups, number % groups
@@ -539,7 +624,6 @@
         )
 
     columns(groups, project)
-    weights_tick(6)
     assemble(1, (0, 1, 2, 3), up_ref)
 
     def second_norm(at):
@@ -549,10 +633,6 @@
 
     by_rows(second_norm)
     mark("gather_end")
-    if second_weight.last < 6:
-        weights_tick(second_weight.last)
-    weights_tick(7)
-    weights_tick(8)
     second_weight.end()
     third_weight.end()
 
@@ -560,7 +640,8 @@
         return Scatter(p, wires, scatter_refs[11 * number : 11 * number + 11], pieces, axis)
 
     scatter_down = scatter(0, p.rings, "y")
-    scatter_up = scatter(1, p.rings + 1, "x")
+    scatter_up = scatter(1, p.rings, "x")
+    scatter_proj = scatter(6, 1, "x")
     scatter_query = [scatter(2, 1, "y"), scatter(3, 1, "x")]
     scatter_value = [scatter(4, 1, "x"), scatter(5, 1, "y")]
     every = slice(None)
@@ -619,7 +700,7 @@
         for i, j, window, quarter, down, over in shifted_blocks():
             first = TOK * window + QUAD * quarter
             block = source[pl.ds(first, PADQ)].astype(BF16)
-            target = out_field.at[(i + 1) % 4, (j + 1) % 4, kind]
+            target = outs[kind].at[(i + 1) % 4, (j + 1) % 4]
             if down or over:
                 place = back.at[number, kind]
                 place[...] = block
@@ -633,6 +714,7 @@
     send_back(result, 0)
     lax.fori_loop(0, p.rings, trade_all, 0)
     scatter_down.cross()
+    scatter_up.cross()
 
     def raise_back(first, number):
         share = p.rings // groups
@@ -660,7 +742,7 @@
 
     def project_back(first, number):
         grad = tn(attended[...], grad_low[:, pl.ds(first, GROUP)])
-        scatter_up.put(across(pl.multiple_of(hid + first, GROUP), GROUP), split_columns(grad))
+        scatter_proj.put(across(first, GROUP), split_columns(grad))
         share = p.rings // groups
         proj_rows = one[pl.ds(number * share, share), :, :, :, pl.ds(3 * width, width)]
         grad_attended[:, pl.ds(first, GROUP)] = nt(
@@ -669,7 +751,8 @@
 
     mark("project_back")
     columns(groups, project_back)
-    scatter_up.trade(across(hid, width), p.rings)
+    full = (every, every, every, every)
+    scatter_proj.trade(full, 0)
 
     def attend_back(group, turns, number, _):
         window = number
@@ -714,11 +797,9 @@
         grad = tn(hidden_one[...], grad_packed[:, first : first + GROUP])
         scatter_value[group].put(across(0, GROUP), split_columns(grad))
 
-    full = (every, every, every, every)
-
-    def up_cross():
-        scatter_up.traded(across(hid, width), p.rings)
-        scatter_up.cross()
+    def proj_cross():
+        scatter_proj.traded(full, 0)
+        scatter_proj.cross()
 
     def packed_cross(group):
         scatter_query[group].traded(full, 0)
@@ -727,9 +808,11 @@
         scatter_value[group].cross()
 
     turns_one = [[] for _ in range(8)]
-    turns_one[2].append(up_cross)
+    turns_one[2].append(proj_cross)
     turns_two = [[] for _ in range(8)]
-    turns_two[1].append(scatter_down.crossed)
+    turns_two[0].append(scatter_down.crossed)
+    turns_two[1].append(scatter_up.crossed)
+    turns_two[5].append(scatter_proj.crossed)
     turns_two[3].append(functools.partial(packed_cross, 0))
 
     mark("attend_back")
@@ -742,7 +825,9 @@
     lax.fori_loop(0, 4, functools.partial(attend_back, 1, turns_two), 0)
     mark("pack_back_two")
     pack_back(1)
-    scatter_up.crossed()
+    scatter_down.spread()
+    for early in (scatter_query[0], scatter_value[0]):
+        early.crossed()
 
     def unpack(first, number):
         share = p.rings // groups
@@ -752,7 +837,6 @@
         )
 
     columns(groups, unpack)
-    scatter_down.spread()
 
     def first_back(at):
         normed, inverse = layer_norm(x_ref[at])
@@ -775,21 +859,22 @@
     scatter_value[1].traded(full, 0)
     scatter_value[1].cross()
     mark("last")
-    for early in (scatter_query[0], scatter_value[0]):
-        early.crossed()
+    scatter_up.spread()
+    scatter_proj.spread()
     scatter_down.collect()
-    scatter_up.spread()
     scatter_query[0].spread()
     scatter_value[0].spread()
     scatter_query[1].crossed()
     scatter_value[1].crossed()
     scatter_down.end()
     scatter_up.collect()
+    scatter_proj.collect()
     scatter_query[0].collect()
     scatter_value[0].collect()
     scatter_query[1].spread()
     scatter_value[1].spread()
     scatter_up.end()
+    scatter_proj.end()
     scatter_query[0].end()
     scatter_value[0].end()
 
@@ -804,9 +889,8 @@
             out_one[:, 4 * width :] = value[:, GROUP : GROUP + 128]
 
     out_three[...] = scatter_down.columns()
-    value = scatter_up.columns()
-    out_two[...] = value[:, :hid]
-    out_one[:, 3 * width : 4 * width] = value[:, hid:]
+    out_two[...] = scatter_up.columns()
+    out_one[:, 3 * width : 4 * width] = scatter_proj.columns()
     write_packed(0)
     mark("collect_last")
     scatter_query[1].collect()
@@ -816,7 +900,7 @@
         if down or over:
             for kind in range(2):
                 wires.landed(
-                    out_field.at[(i + 1) % 4, (j + 1) % 4, kind],
+                    outs[kind].at[(i + 1) % 4, (j + 1) % 4],
                     returns + 7 * kind + number,
                     beyond(down, over, -1),
                 )
@@ -859,21 +943,13 @@
     start = (
         cells.astype(F32) + land[:, :, None].astype(F32) * land_embed[None, None, :]
     ).astype(BF16)
-    field = jnp.stack([blocks_of(start), blocks_of(cotangent)], axis=2)
     rows, hid = up_weight.shape
     width = cells.shape[2]
     deep = down_weight.shape[0]
     tokens = 4 * TOK
     rings = lons // 4
-    shard_one = jnp.concatenate(
-        [
-            qkv_weight,
-            proj_weight,
-            jnp.broadcast_to(gain_one[:, None], (rows, 64)),
-            jnp.broadcast_to(gain_two[:, None], (rows, 64)),
-        ],
-        axis=1,
-    )
+    first = lax.broadcasted_iota(jnp.int32, (rows, 128), 1) < 64
+    shard_gain = jnp.where(first, gain_one[:, None], gain_two[:, None])
 
     def scatter_scratch(lines, across):
         quarter = across // 4
@@ -911,36 +987,46 @@
         pltpu.VMEM((tokens, 3 * width), BF16),
         pltpu.VMEM((16, width), F32),
         pltpu.VMEM((16, width), F32),
+        pltpu.VMEM((rows, 4 * width + 128), BF16),
         pltpu.VMEM((rings, 2, 2, rows, 4 * width + 128), BF16),
         pltpu.VMEM((rings, 2, 2, rows, hid), BF16),
         pltpu.VMEM((rings, 2, 2, deep, width), BF16),
     ]
     scratch += scatter_scratch(deep, width)
-    scratch += scatter_scratch(rows, hid + width)
-    for _ in range(4):
+    scratch += scatter_scratch(rows, hid)
+    for _ in range(5):
         scratch += scatter_scratch(rows, 2 * GROUP)
-    wires = 14 + 14 + 3 * (3 * rings - 1) + 6 * (rings - 1 + 9) + 2 * rings + 5
+    wires = 14 + 14 + 3 * (3 * rings - 1) + 6 + 7 * (rings - 1 + 9) + 2 * rings + 5
     scratch += [pltpu.SemaphoreType.DMA((wires,)), pltpu.SemaphoreType.DMA((wires,))]
     vmem = pl.BlockSpec(memory_space=pltpu.VMEM)
-    out_field, one, two, three = pl.pallas_call(
+    block_out, grad_cells, one, two, three = pl.pallas_call(
         functools.partial(kernel, lats, lons),
         out_shape=(
-            jax.ShapeDtypeStruct((4, 4, 2, PADQ, width), BF16),
+            jax.ShapeDtypeStruct((4, 4, PADQ, width), BF16),
+            jax.ShapeDtypeStruct((4, 4, PADQ, width), BF16),
             jax.ShapeDtypeStruct((rows, 4 * width + 128), F32),
             jax.ShapeDtypeStruct((rows, hid), F32),
             jax.ShapeDtypeStruct((deep, width), F32),
         ),
-        in_specs=[vmem] * 4,
-        out_specs=(vmem,) * 4,
+        in_specs=[vmem] * 7,
+        out_specs=(vmem,) * 5,
         scratch_shapes=scratch,
         compiler_params=pltpu.CompilerParams(
             collective_id=0, has_side_effects=True, vmem_limit_bytes=63 * 2**20
         ),
         name="block",
-    )(field, shard_one, up_weight, down_weight)
+    )(
+        blocks_of(start),
+        blocks_of(cotangent),
+        qkv_weight,
+        proj_weight,
+        shard_gain,
+        up_weight,
+        down_weight,
+    )
     return (
-        field_of(out_field[:, :, 0]),
-        field_of(out_field[:, :, 1]),
+        field_of(block_out),
+        field_of(grad_cells),
         one[:, : 3 * width],
         one[:, 3 * width : 4 * width],
         two,

time: 150 us -> 147 us (0.980)
  local copies, waits for them, and re-layouts: 13.3 us -> 11.6 us
    pad x0 -> x2, local copies, waits for them, and re-layouts: none -> 1.96 us  [blocks_of(): return jnp.pad(shaped, ((0, 0), (0, 0), (0, PADQ - QUAD), (0, 0)))]
    concatenate x1 -> x0, local copies, waits for them, and re-layouts: 1.51 us -> none  [body(): jnp.concatenate([qkv_weight, proj_weight, jnp.broadcast_to(gain_one[:, No...]
where the time goes in v4:
time: 147 us
  Pallas kernels  131 us (89%)
  local copies, waits for them, and re-layouts  11.6 us (8%)
  other arithmetic  3.32 us (2%)
    pallas_call x1, Pallas kernels, body(): pl.pallas_call(functools.partial(kernel, lats, lons), out_shape=(jax.Shap...  131 us

profile of v4, /device:TPU:32, one launch (start us, length us, event | category | flops | bytes accessed | tf_op | source)
XLA Modules:
  0.0 146.8 jit_solution(14577057674656116174)
XLA Ops:
  0.6 1.3 broadcast_select_fusion.gain_shard
  2.0 0.7 convert_element_type.14
  2.7 1.3 add_convert_fusion
  4.0 0.2 reshape.45
  4.2 0.3 copy.22
  4.5 0.1 copy.23
  4.6 0.0 copy-start
  4.6 1.0 pad.7.cells_in
  5.6 0.2 copy-done
  5.8 0.2 reshape.47
  6.0 0.3 copy.24
  6.3 0.1 copy.25
  6.4 1.0 pad.8.cotangent_in
  7.4 131.1 %block.1 = (bf16[4,4,48,512]{3,2,1,0:T(8,128)(2,1)}, bf16[4,4,48,512]{3,2,1,0:T(8,128)(2,1)}, f32[16,2176]{1,0:T(8,128)}, f32[16,2048]{1,0:T(8,128)}, f32[64,512]{1,0:T(8,128)}) custom-call(bf16[4,4,48,512]{3,2,1,0:T(8,128)(2,1)} %pad.7.cells_in, bf16[4,4,48,512]{3,2,1,0:T(8,128)(2,1)} %pad.8.cotangent_in, bf16[16,1536]{1,0:T(8,128)(2,1)} %qkv_shard.1, ...), custom_call_target="tpu_custom_call" | custom-call | tf_op jit(solution)/shard_map/block/pallas_call | solution.py:1002
  138.5 1.1 slice.18
  139.7 0.0 copy-start.2
  139.7 0.3 copy.26
  140.0 0.6 copy-done.2
  140.6 0.7 slice_reduce_fusion
  141.3 0.6 slice.21
  141.9 0.6 slice.20
  142.5 0.2 copy.27
  142.7 0.0 copy-start.1
  142.7 1.0 reshape.50
  143.7 0.2 copy-done.1
  143.9 0.3 copy.28
  144.3 0.2 copy.29
  144.4 0.0 copy-start.4
  144.4 0.0 copy-start.3
  144.4 1.0 reshape.52
  145.5 0.0 copy-done.4
  145.5 0.7 copy.32
  146.1 0.0 copy-done.3
  146.1 0.7 copy.33
  (2 shorter events, 0.1 us)
Async XLA Ops:
  4.6 1.2 copy-start
  139.7 0.9 copy-start.2
  142.7 1.2 copy-start.1
  144.4 1.0 copy-start.4
  144.4 1.7 %copy-start.3 = (f32[64,512]{1,0:T(8,128)S(1)}, f32[64,512]{1,0:T(8,128)}, u32[]{:S(2)}) copy-start(f32[64,512]{1,0:T(8,128)} %get-tuple-element.33) | copy-start | bytes 393220

commit v5 on v4

--- a/solution.py
+++ b/solution.py
@@ -810,9 +810,9 @@
     turns_one = [[] for _ in range(8)]
     turns_one[2].append(proj_cross)
     turns_two = [[] for _ in range(8)]
-    turns_two[0].append(scatter_down.crossed)
-    turns_two[1].append(scatter_up.crossed)
-    turns_two[5].append(scatter_proj.crossed)
+    turns_two[2].append(scatter_down.crossed)
+    turns_two[4].append(scatter_up.crossed)
+    turns_two[7].append(scatter_proj.crossed)
     turns_two[3].append(functools.partial(packed_cross, 0))
 
     mark("attend_back")
@@ -825,7 +825,6 @@
     lax.fori_loop(0, 4, functools.partial(attend_back, 1, turns_two), 0)
     mark("pack_back_two")
     pack_back(1)
-    scatter_down.spread()
     for early in (scatter_query[0], scatter_value[0]):
         early.crossed()
 
@@ -837,6 +836,7 @@
         )
 
     columns(groups, unpack)
+    scatter_down.spread()
 
     def first_back(at):
         normed, inverse = layer_norm(x_ref[at])

time: 147 us -> 146 us (level)
  Pallas kernels: 131 us -> 129 us
    pallas_call x1, Pallas kernels: 131 us -> 129 us  [body(): pl.pallas_call(functools.partial(kernel, lats, lons), out_shape=(jax.Shap...]
where the time goes in v5:
time: 146 us; the launch traced here: 145 us
  Pallas kernels  129 us (88%)
  local copies, waits for them, and re-layouts  11.6 us (8%)
  other arithmetic  3.32 us (2%)
    pallas_call x1, Pallas kernels, body(): pl.pallas_call(functools.partial(kernel, lats, lons), out_shape=(jax.Shap...  129 us

profile of v5, /device:TPU:32, one launch (start us, length us, event | category | flops | bytes accessed | tf_op | source)
XLA Modules:
  0.0 145.0 jit_solution(8369519822628138107)
XLA Ops:
  0.6 1.3 broadcast_select_fusion.gain_shard
  2.0 0.7 convert_element_type.14
  2.7 1.3 add_convert_fusion
  4.0 0.2 reshape.45
  4.2 0.3 copy.22
  4.5 0.1 copy.23
  4.6 0.0 copy-start
  4.6 1.0 pad.7.cells_in
  5.6 0.2 copy-done
  5.8 0.2 reshape.47
  6.0 0.3 copy.24
  6.3 0.1 copy.25
  6.4 1.0 pad.8.cotangent_in
  7.4 129.3 %block.1 = (bf16[4,4,48,512]{3,2,1,0:T(8,128)(2,1)}, bf16[4,4,48,512]{3,2,1,0:T(8,128)(2,1)}, f32[16,2176]{1,0:T(8,128)}, f32[16,2048]{1,0:T(8,128)}, f32[64,512]{1,0:T(8,128)}) custom-call(bf16[4,4,48,512]{3,2,1,0:T(8,128)(2,1)} %pad.7.cells_in, bf16[4,4,48,512]{3,2,1,0:T(8,128)(2,1)} %pad.8.cotangent_in, bf16[16,1536]{1,0:T(8,128)(2,1)} %qkv_shard.1, ...), custom_call_target="tpu_custom_call" | custom-call | tf_op jit(solution)/shard_map/block/pallas_call | solution.py:1002
  136.8 1.1 slice.18
  137.9 0.0 copy-start.2
  137.9 0.3 copy.26
  138.2 0.6 copy-done.2
  138.8 0.7 slice_reduce_fusion
  139.5 0.6 slice.21
  140.1 0.6 slice.20
  140.8 0.2 copy.27
  140.9 0.0 copy-start.1
  141.0 1.0 reshape.50
  142.0 0.2 copy-done.1
  142.2 0.3 copy.28
  142.5 0.2 copy.29
  142.7 0.0 copy-start.4
  142.7 0.0 copy-start.3
  142.7 1.0 reshape.52
  143.7 0.0 copy-done.4
  143.7 0.7 copy.32
  144.3 0.0 copy-done.3
  144.4 0.7 copy.33
  (2 shorter events, 0.1 us)
Async XLA Ops:
  4.6 1.2 copy-start
  137.9 0.9 copy-start.2
  140.9 1.2 copy-start.1
  142.7 1.0 copy-start.4
  142.7 1.7 %copy-start.3 = (f32[64,512]{1,0:T(8,128)S(1)}, f32[64,512]{1,0:T(8,128)}, u32[]{:S(2)}) copy-start(f32[64,512]{1,0:T(8,128)} %get-tuple-element.33) | copy-start | bytes 393220
